TPU v7x, 256 devices: a whole 4x4x8 slice. The times are simulated.
256 devices in a mesh: row: 8 (over z_hi, y), col: 32 (over x, z_lo, core).
Axes of the slice: x: 4, y: 4, z: 8 (z_hi: 2, z_lo: 4; z = z_hi * 4 + z_lo), core: 2. Of those that a mesh axis runs over, the one named last changes fastest.
Arguments:
- row_feats: bfloat16 [64, 8192], P(None, ('row', 'col')), may hold values from -0.75 to 0.75
- row_alpha: bfloat16 [8192], P(('row', 'col')), may hold values from -18 to 18
- row_solves: bfloat16 [32, 8192], P(None, ('row', 'col')), may hold values from -288 to 288
- col_feats: bfloat16 [64, 262144], P('row', 'col'), may hold values from -0.75 to 0.75
- col_alpha: bfloat16 [262144], P('col'), may hold values from -18 to 18
- col_weight: float32 [262144], P('col'), may hold values from 0.02 to 0.25
- col_probes: bfloat16 [32, 262144], P('row', 'col'), may hold values from -6 to 6
Outputs:
- grad_rows: float32 [64, 8192], P(None, ('row', 'col'))
- grad_cols: float32 [64, 262144], P('row', 'col')
All inputs are finite; a program needn't handle non-finite values.
Results may differ from a plain program's by a relative error of at most 0.0075.
Values may be sent and summed in bfloat16 or wider, within the bound.
A program may use at most 64 MiB of HBM per device.

v0:
```python
import math

import jax
import jax.numpy as jnp
from jax import lax
from jax.sharding import PartitionSpec as P


def tile_terms(row_feats, left, sq_row, col_feats, right, sq_col):
    contract = (((0,), (0,)), ((), ()))
    cross = lax.dot_general(row_feats, col_feats, contract, preferred_element_type=jnp.float32)
    kernel = jnp.exp(-(sq_row[:, None] + sq_col[None, :] - 2.0 * cross) * 0.5)
    weight = lax.dot_general(left, right, contract, preferred_element_type=jnp.float32)
    product = (weight * kernel).astype(jnp.bfloat16)
    row_sum = jnp.sum(product.astype(jnp.float32), axis=1)
    col_sum = jnp.sum(product.astype(jnp.float32), axis=0)
    toward_row = lax.dot_general(
        col_feats, product, (((1,), (1,)), ((), ())), preferred_element_type=jnp.float32
    )
    toward_col = jnp.dot(row_feats, product, preferred_element_type=jnp.float32)
    part_row = toward_row - row_sum[None, :] * row_feats.astype(jnp.float32)
    part_col = toward_col - col_sum[None, :] * col_feats.astype(jnp.float32)
    return (part_row, part_col)


def sweep(row_feats, row_alpha, row_solves, col_feats, col_alpha, col_weight, col_probes):
    feat_count = row_feats.shape[0]
    row_count = row_feats.shape[1]
    col_count = col_feats.shape[1]
    probe_count = col_probes.shape[0]
    left = jnp.concatenate([row_alpha[None, :], row_solves], axis=0)
    sq_row = jnp.sum(jnp.square(row_feats.astype(jnp.float32)), axis=0)
    probe_part = -0.5 / probe_count * col_weight[None, :] * col_probes.astype(jnp.float32)
    right = jnp.concatenate(
        [0.5 * col_alpha.astype(jnp.float32)[None, :], probe_part], axis=0
    ).astype(jnp.bfloat16)
    sq_col = jnp.sum(jnp.square(col_feats.astype(jnp.float32)), axis=0)
    target = max(1, 2097152 // row_count)
    width = math.gcd(col_count, target)
    blocks = col_count // width

    def one_block(step, carry):
        total_row, total_col = carry
        start = step * width
        feats = lax.dynamic_slice_in_dim(col_feats, start, width, 1)
        rights = lax.dynamic_slice_in_dim(right, start, width, 1)
        squares = lax.dynamic_slice_in_dim(sq_col, start, width, 0)
        part_row, part_col = tile_terms(row_feats, left, sq_row, feats, rights, squares)
        total_col = lax.dynamic_update_slice_in_dim(total_col, part_col, start, 1)
        return (total_row + part_row, total_col)

    start_row = jnp.zeros((feat_count, row_count), jnp.float32)
    start_col = jnp.zeros((feat_count, col_count), jnp.float32)
    return lax.fori_loop(0, blocks, one_block, (start_row, start_col))


def body(row_feats, row_alpha, row_solves, col_feats, col_alpha, col_weight, col_probes):
    row_size = lax.axis_size("row")
    col_size = lax.axis_size("col")
    window = row_alpha.shape[0] * row_size * col_size
    points = col_alpha.shape[0] * col_size
    row_scale = 1.0 / points**0.5
    col_scale = 1.0 / window**0.5
    feats_rows, alpha_rows, solves_rows = (
        lax.all_gather(row_feats, "col", axis=1, tiled=True),
        lax.all_gather(row_alpha, "col", axis=0, tiled=True),
        lax.all_gather(row_solves, "col", axis=1, tiled=True),
    )
    feats_cols, probes_cols = (
        lax.all_gather(col_feats, "row", axis=0, tiled=True),
        lax.all_gather(col_probes, "row", axis=0, tiled=True),
    )
    part_row, part_col = sweep(
        feats_rows, alpha_rows, solves_rows, feats_cols, col_alpha, col_weight, probes_cols
    )
    grad_rows = lax.psum_scatter(part_row, "col", scatter_dimension=1, tiled=True) * row_scale
    grad_cols = lax.psum_scatter(part_col, "row", scatter_dimension=0, tiled=True) * col_scale
    return (grad_rows, grad_cols)


def solution(mesh):
    in_specs = (
        P(None, ("row", "col")),
        P(("row", "col")),
        P(None, ("row", "col")),
        P("row", "col"),
        P("col"),
        P("col"),
        P("row", "col"),
    )
    out_specs = (P(None, ("row", "col")), P("row", "col"))
    return jax.shard_map(body, mesh=mesh, in_specs=in_specs, out_specs=out_specs, check_vma=False)
```

profile of v0, /device:TPU:2, one launch (start us, length us, event | category | flops | bytes accessed | tf_op | source)
XLA Modules:
  0.0 520.5 jit_solution(4402458551213445483)
XLA Ops:
  7.2 0.0 copy-start.7
  7.2 0.0 all-gather.3.cloned.1.call-start
  7.3 0.7 all-gather.3.cloned.1.call-update
  7.9 0.0 reduce-scatter.3.cloned.1.call-start
  8.0 49.2 %all-gather = bf16[8,4,8192]{2,1,0:T(4,128)(2,1)S(1)} all-gather(bf16[1,4,8192]{2,1,0:T(4,128)(2,1)} %bitcast.39), channel_id=1, replica_groups=mesh['row'=8,'col'=32] {'row'}, dimensions={0}, use_global_device_ids=true | all-gather | bytes 589824 | tf_op jit(solution)/shard_map/all_gather | solution.py:71
  57.2 0.1 reshape.17
  57.3 0.8 broadcast_multiply_fusion.1
  58.0 0.1 multiply_convert_fusion
  58.1 35.6 %all_gather.19 = bf16[64,1024]{0,1:T(8,128)(2,1)S(1)} all-gather(bf16[64,32]{0,1:T(8,128)(2,1)} %param.9), channel_id=1, replica_groups=mesh['row'=8,'col'=32] {'col'}, dimensions={1}, use_global_device_ids=true | all-gather | bytes 135168 | tf_op jit(solution)/shard_map/all_gather | solution.py:65
  93.8 0.1 copy.22
  94.0 0.1 copy.20
  94.0 38.0 %all_gather.18 = bf16[32,1024]{0,1:T(8,128)(2,1)S(1)} all-gather(bf16[32,32]{0,1:T(8,128)(2,1)S(1)} %copy.20), channel_id=1, replica_groups=mesh['row'=8,'col'=32] {'col'}, dimensions={1}, use_global_device_ids=true | all-gather | bytes 67584 | tf_op jit(solution)/shard_map/all_gather | solution.py:67
  132.1 0.1 copy.21
  132.2 0.0 copy-done.7
  132.2 0.6 dynamic-slice
  133.5 0.2 dynamic-update-slice
  133.7 63.3 %all-reduce = bf16[1024]{0:T(1024)(128)(2,1)S(1)} all-reduce(bf16[1024]{0:T(1024)(128)(2,1)S(1)} %dynamic-update-slice), channel_id=1, replica_groups=mesh['row'=8,'col'=32] {'col'}, use_global_device_ids=true, to_apply=%add | all-reduce | flops 1024 | bytes 4096
  197.0 0.7 pad_maximum_fusion.1
  197.7 0.2 multiply_reduce_fusion.1
  197.9 1.0 pad_maximum_fusion
  198.9 2.1 multiply_reduce_fusion
  201.0 0.1 broadcast_in_dim.24
  201.1 55.4 %while.16 = (s32[]{:T(128)}, f32[64,1024]{1,0:T(8,128)S(1)}, f32[64,8192]{1,0:T(8,128)S(1)}, bf16[64,8192]{1,0:T(8,128)(2,1)}, bf16[33,8192]{1,0:T(8,128)(2,1)},...) while((s32[]{:T(128)}, f32[64,1024]{1,0:T(8,128)S(1)}, ...), condition=%wide.region_5.0_spmd.clone, body=%wide.region_2.0_spmd.clone.sunk | while | flops 965407744 | bytes 53115164 | solution.py:54
  201.2 0.0 copy-start.3
  201.2 2.3 fusion.37
  203.4 0.7 dynamic_slice.42
  204.1 4.4 convert_reduce_fusion.3
  208.6 1.9 copy-done
  210.5 0.0 copy-done.1
  210.5 1.4 fusion.39
  211.9 3.1 fusion.38
  215.0 0.0 copy-start.3
  215.0 2.3 fusion.37
  217.3 0.7 dynamic_slice.42
  218.0 4.4 convert_reduce_fusion.3
  222.4 0.0 copy-start
  222.5 1.9 copy-done
  224.4 1.4 fusion.39
  225.8 3.1 fusion.38
  228.9 0.0 copy-start.3
  228.9 2.3 fusion.37
  231.1 0.7 dynamic_slice.42
  231.8 0.0 copy-done.3
  231.8 4.4 convert_reduce_fusion.3
  236.3 1.9 copy-done
  238.2 1.4 fusion.39
  239.6 3.1 fusion.38
  242.7 0.0 copy-start.3
  242.7 2.3 fusion.37
  245.0 0.7 dynamic_slice.42
  245.7 4.4 convert_reduce_fusion.3
  250.2 0.0 copy-start
  250.2 1.9 copy-done
  252.1 1.4 fusion.39
  253.5 3.1 fusion.38
  256.6 1.2 copy.23
  257.8 0.0 reduce-scatter.3.cloned.1.call-update
  257.8 0.0 reduce-scatter.5.cloned.1.call-start
  257.8 0.2 copy-done.2
  258.1 0.4 reduce-scatter.5.cloned.1.call-update
  258.5 137.3 %reduce-scatter.3.cloned.1.call-done = f32[64,32]{0,1:T(8,128)} async-done(((f32[64,1024]{0,1:T(8,128)}), f32[64,32]{0,1:T(8,128)}) %reduce-scatter.3.cloned.1.call-update) | async-done | bytes 8208 | tf_op jit(solution)/shard_map/reduce_scatter | solution.py:76
  395.8 1.3 broadcast_multiply_fusion.2
  397.1 115.2 %reduce-scatter.5.cloned.1.call-done = f32[8,8192]{1,0:T(8,128)} async-done(((f32[64,8192]{1,0:T(8,128)}), f32[8,8192]{1,0:T(8,128)}) %reduce-scatter.5.cloned.1.call-update) | async-done | bytes 262160 | tf_op jit(solution)/shard_map/reduce_scatter | solution.py:77
  512.3 1.7 broadcast_multiply_fusion
  (25 shorter events, 0.1 us)
Async XLA Ops:
  7.2 125.0 %copy-start.7 = (u32[256]{0:T(256)S(1)}, u32[256]{0:T(256)}, u32[]{:S(2)}) copy-start(u32[256]{0:T(256)} %constant.66) | copy-start | bytes 3076
  7.2 86.7 %copy-start.4 = (bf16[8192]{0:T(1024)(128)(2,1)S(1)}, bf16[8192]{0:T(1024)(128)(2,1)}, u32[]{:S(2)}) copy-start(bf16[8192]{0:T(1024)(128)(2,1)} %param.13) | copy-start | bytes 49156
  7.2 86.8 %copy-start.5 = (bf16[32,32]{1,0:T(8,128)(2,1)S(1)}, bf16[32,32]{1,0:T(8,128)(2,1)}, u32[]{:S(2)}) copy-start(bf16[32,32]{1,0:T(8,128)(2,1)} %param.11) | copy-start | bytes 6148
  7.2 126.3 %copy-start.6 = (bf16[32]{0:T(256)(128)(2,1)S(1)}, bf16[32]{0:T(256)(128)(2,1)}, u32[]{:S(2)}) copy-start(bf16[32]{0:T(256)(128)(2,1)} %param.10) | copy-start | bytes 196
  7.2 191.7 %all-gather.3.cloned.1.call-start = ((), (), s32[]{:S(2)}) async-start(), calls=%async_computation.2 | async-start | bytes 1179648 | tf_op jit(solution)/shard_map/all_gather | solution.py:70
  7.9 387.9 %reduce-scatter.3.cloned.1.call-start = ((), (), s32[]{:S(2)}) async-start(), calls=%async_computation.3 | async-start | bytes 540672 | tf_op jit(solution)/shard_map/reduce_scatter | solution.py:76
  201.2 3.0 copy-start.3
  204.1 6.4 %copy-start.1 = (bf16[64,8192]{1,0:T(8,128)(2,1)S(1)}, bf16[64,8192]{1,0:T(8,128)(2,1)}, u32[]{:S(2)}) copy-start(bf16[64,8192]{1,0:T(8,128)(2,1)} %get-tuple-element.327) | copy-start | bytes 3145732 | tf_op jit(solution)/shard_map/while
  208.6 1.9 copy-start
  215.0 3.0 copy-start.3
  218.0 6.4 %copy-start.1 = (bf16[64,8192]{1,0:T(8,128)(2,1)S(1)}, bf16[64,8192]{1,0:T(8,128)(2,1)}, u32[]{:S(2)}) copy-start(bf16[64,8192]{1,0:T(8,128)(2,1)} %get-tuple-element.327) | copy-start | bytes 3145732 | tf_op jit(solution)/shard_map/while
  222.4 1.9 copy-start
  228.9 3.0 copy-start.3
  231.8 6.4 %copy-start.1 = (bf16[64,8192]{1,0:T(8,128)(2,1)S(1)}, bf16[64,8192]{1,0:T(8,128)(2,1)}, u32[]{:S(2)}) copy-start(bf16[64,8192]{1,0:T(8,128)(2,1)} %get-tuple-element.327) | copy-start | bytes 3145732 | tf_op jit(solution)/shard_map/while
  236.3 1.9 copy-start
  242.7 3.0 copy-start.3
  245.7 6.4 %copy-start.1 = (bf16[64,8192]{1,0:T(8,128)(2,1)S(1)}, bf16[64,8192]{1,0:T(8,128)(2,1)}, u32[]{:S(2)}) copy-start(bf16[64,8192]{1,0:T(8,128)(2,1)} %get-tuple-element.327) | copy-start | bytes 3145732 | tf_op jit(solution)/shard_map/while
  250.2 1.9 copy-start
  256.6 1.5 copy-start.2
  257.8 254.6 %reduce-scatter.5.cloned.1.call-start = ((), (), s32[]{:S(2)}) async-start(), calls=%async_computation.4 | async-start | bytes 2359296 | tf_op jit(solution)/shard_map/reduce_scatter | solution.py:77
Sparse Core Ops, SparseCore 0:
  10.7 66.4 all-gather.2
  257.9 137.8 reduce-scatter.2
  400.4 111.8 reduce-scatter.4
where the time goes:
time: 521 us
  waiting for transfers between devices  254 us (49%)
  blocking collectives  186 us (36%)
  matrix products  44.6 us (9%)
  between operations  14.5 us (3%)
  local copies, waits for them, and re-layouts  13.4 us (3%)
  other arithmetic  7.81 us (1%)
    reduce_scatter x1, waiting for transfers between devices, body(): lax.psum_scatter(part_row, 'col', scatter_dimension=1, tiled=True)  137 us
    reduce_scatter x1, waiting for transfers between devices, body(): lax.psum_scatter(part_col, 'row', scatter_dimension=0, tiled=True)  115 us
    unnamed x1, blocking collectives  63.3 us
    all_gather x1, blocking collectives, body(): lax.all_gather(col_probes, 'row', axis=0, tiled=True)  49.2 us
    all_gather x1, blocking collectives, body(): lax.all_gather(row_solves, 'col', axis=1, tiled=True)  38 us
    all_gather x1, blocking collectives, body(): lax.all_gather(row_feats, 'col', axis=1, tiled=True)  35.6 us
    dot_general x4, matrix products, tile_terms(): lax.dot_general(left, right, contract, preferred_element_type=jnp.float32)  17.8 us
    dot_general x4, matrix products, tile_terms(): lax.dot_general(col_feats, product, (((1,), (1,)), ((), ())), preferred_e...  12.3 us
  transfers between devices with their start and end apart: 3, of which 2 were waited for; matrix products, arithmetic and copies ran while one was open for 1% of the time, Pallas kernels for 0%

commit v1 on v0

v1 whole, which is shorter than its diff:
```python
import functools

import jax
import jax.numpy as jnp
from jax import lax
from jax.experimental import pallas as pl
from jax.experimental.pallas import tpu as pltpu
from jax.sharding import PartitionSpec as P

MESH = pl.DeviceIdType.MESH
F32 = jnp.float32
BF16 = jnp.bfloat16

FEAT = 64
PROBES = 32
NX, NY, NZ = 4, 4, 8
TILE = 1024
ITEM = 512

ORDER = (
    (0, 0, 0), (0, 0, 1), (0, 1, 0),
    (1, 0, 0), (1, 0, 1), (1, 1, 0), (1, 1, 1),
    (3, 0, 0), (3, 0, 1), (3, 1, 0), (3, 1, 1),
    (2, 0, 0), (2, 0, 1), (2, 1, 0), (2, 1, 1),
    (0, 1, 1),
)


def look(values, at):
    out = jnp.int32(values[0])
    for k, v in enumerate(values[1:], 1):
        out = jnp.where(at == k, jnp.int32(v), out)
    return out


def parts3(v):
    hi = v.astype(BF16).astype(F32)
    mid = (v - hi).astype(BF16).astype(F32)
    return hi, mid, v - hi - mid


def kernel(
    row_scale, col_scale,
    rf_ref, ra_ref, rs_ref, cf_ref, ca_ref, cw_ref, cp_ref,
    out_rows, out_cols,
    rows, send_cols, recv_cols, cx, cr, xct, acc_col, acc_row, part, got,
    y_out, y_in, z_out, z_in, back_out, back_in,
    col_s, col_r, z_s, z_r, y_s, y_r, g_s, g_r, f_s,
    part_s, part_r, yy_s, yy_r, zz_s, zz_r, back_s, back_r,
):
    row = lax.axis_index("row")
    col = lax.axis_index("col")
    y, core = row % 4, col % 2
    x, z = col // 8, (row // 4) * 4 + (col // 2) % 4

    def at(px, py, pz, pc):
        return {"row": (pz // 4) * 4 + py, "col": (px * 4 + pz % 4) * 2 + pc}

    def z_peer(d):
        return at(x, y, (z + d) % NZ, core)

    def y_peer(d):
        return at(x, (y + d) % NY, z, core)

    def row_peer(d):
        return {"row": (row + d) % 8, "col": col}

    barrier = pltpu.get_barrier_semaphore()
    peers = [z_peer(d) for d in range(1, NZ)] + [y_peer(d) for d in range(1, NY)]
    peers += [at((x + d) % NX, y, z, core) for d in range(1, NX)]
    peers += [at((x + d) % NX, y, z, 1 - core) for d in range(NX)]
    peers += [at(x, (y + d) % NY, (z + 4) % NZ, core) for d in range(1, NY)]
    for peer in peers:
        pl.semaphore_signal(barrier, inc=1, device_id=peer, device_id_type=MESH)

    rf = rf_ref[...].astype(F32)
    n = rf.shape[1]
    sq = -0.5 * jnp.sum(rf * rf, axis=0, keepdims=True)
    one = jnp.ones((1, n), F32)
    mine = jnp.concatenate(
        [rf, one, one, one, *parts3(sq), ra_ref[...].astype(F32), jnp.zeros((1, n), F32),
         rs_ref[...].astype(F32), jnp.zeros((24, n), F32)], axis=0)
    mine = jnp.concatenate([mine, jnp.zeros((128, 128 - n), F32)], axis=1)
    me_g = x * 2 + core
    rows[me_g, y, z] = mine.T[:n].astype(BF16)

    for p in range(8):
        feats = cf_ref[:, p * TILE:(p + 1) * TILE].astype(F32)
        probes = cp_ref[:, p * TILE:(p + 1) * TILE].astype(F32)
        left = jnp.concatenate([feats[:, :512], feats[:, 512:]], axis=0)
        right = jnp.concatenate([probes[:, q * 256:(q + 1) * 256] for q in range(4)], axis=0)
        send_cols[p] = jnp.concatenate([left, right], axis=1).astype(BF16)

    pl.semaphore_wait(barrier, len(peers))

    def z_copy(d):
        return pltpu.make_async_remote_copy(
            src_ref=rows.at[me_g, y, z], dst_ref=rows.at[me_g, y, z],
            send_sem=z_s.at[d], recv_sem=z_r.at[d], device_id=z_peer(d), device_id_type=MESH)

    def col_copy(d):
        return pltpu.make_async_remote_copy(
            src_ref=send_cols.at[(row + d) % 8], dst_ref=recv_cols.at[row],
            send_sem=col_s.at[d], recv_sem=col_r.at[d], device_id=row_peer(d), device_id_type=MESH)

    def y_copy(d):
        return pltpu.make_async_remote_copy(
            src_ref=rows.at[me_g, y], dst_ref=rows.at[me_g, y],
            send_sem=y_s.at[d], recv_sem=y_r.at[d], device_id=y_peer(d), device_id_type=MESH)

    def g_copy(g, d, peer, send_sem):
        return pltpu.make_async_remote_copy(
            src_ref=rows.at[g], dst_ref=rows.at[g],
            send_sem=send_sem.at[d], recv_sem=g_r.at[g], device_id=peer, device_id_type=MESH)

    def x_copy(d):
        return g_copy(me_g, d, at((x + d) % NX, y, z, core), g_s)

    def core_copy(g, d):
        return g_copy(g, d, at(x, y, z, 1 - core), f_s)

    z_copies = [z_copy(d) for d in range(1, NZ)]
    for c in z_copies:
        c.start()
    col_copies = [col_copy(d) for d in range(1, 8)]
    for c in col_copies:
        c.start()
    recv_cols[row] = send_cols[row]
    for c in z_copies:
        c.wait_recv()
    y_copies = [y_copy(d) for d in range(1, NY)]
    for c in y_copies:
        c.start()
    for c in y_copies:
        c.wait_recv()
    x_copies = [x_copy(d) for d in (1, 3, 2)] + [core_copy(me_g, 0)]
    for c in x_copies:
        c.start()
    for c in col_copies:
        c.wait_recv()

    feats = jnp.concatenate(
        [jnp.concatenate([recv_cols[p, 0:16, 0:512].astype(F32)[8 * h:8 * h + 8] for h in range(2)], axis=1)
         for p in range(8)], axis=0)
    probes = []
    for p in range(8):
        block = recv_cols[p, 0:16, 512:768].astype(F32)
        probes.append(jnp.concatenate([block[4 * q:4 * q + 4] for q in range(4)], axis=1))
    probes = jnp.concatenate(probes, axis=0)
    mask = lax.broadcasted_iota(jnp.int32, (8, TILE), 0) == row
    weight = jnp.sum(jnp.where(mask, cw_ref[...], 0.0), axis=0, keepdims=True)
    alpha = jnp.sum(jnp.where(mask, ca_ref[...].astype(F32), 0.0), axis=0, keepdims=True)
    sq = -0.5 * jnp.sum(feats * feats, axis=0, keepdims=True)
    one = jnp.ones((1, TILE), F32)
    none = jnp.zeros((1, TILE), F32)
    cx[...] = jnp.concatenate(
        [feats, *parts3(sq), one, one, one, none, none, jnp.zeros((56, TILE), F32)], axis=0).astype(BF16)
    cr[...] = jnp.concatenate(
        [jnp.zeros((70, TILE), F32), 0.5 * alpha, none, (-0.5 / PROBES) * weight * probes,
         jnp.zeros((24, TILE), F32)], axis=0).astype(BF16)
    xct[...] = jnp.concatenate(
        [feats, one, jnp.zeros((63, TILE), F32)], axis=0).T.astype(BF16)

    acc_col[...] = jnp.zeros_like(acc_col)
    lane = lax.broadcasted_iota(jnp.int32, (ITEM // 2, 128), 1)

    def part_copy(s, dx, dc):
        return pltpu.make_async_remote_copy(
            src_ref=part.at[s], dst_ref=got.at[s], send_sem=part_s.at[s], recv_sem=part_r.at[s],
            device_id=at((x + dx) % NX, y, z, (core + dc) % 2), device_id_type=MESH)

    def item(s, _):
        dx = look([o[0] for o in ORDER], s)
        dc = look([o[1] for o in ORDER], s)
        half = look([o[2] for o in ORDER], s)
        first = jnp.logical_and(s >= 2, jnp.logical_and(half == 0, True))
        g = ((x + dx) % NX) * 2 + (core + dc) % 2

        @pl.when(first)
        def _():
            core_copy(g, 0).wait_recv()

        @pl.when(jnp.logical_and(first, dc == 0))
        def _():
            core_copy(g, dx).start()

        r = rows[g, pl.ds(half * 2, 2)].reshape(ITEM, 128)
        cross = jnp.dot(r, cx[...], preferred_element_type=F32)
        weights = jnp.dot(r, cr[...], preferred_element_type=F32)
        prod = (weights * jnp.exp(cross)).astype(BF16)
        t = jnp.dot(prod, xct[...], preferred_element_type=F32)
        acc_col[...] += jnp.dot(r.T[0:80], prod, preferred_element_type=F32)
        t = t - t[:, 64:65] * r.astype(F32)
        t = t.reshape(ITEM // 32, 2, 16, 128)
        lo = t[:, 0].reshape(ITEM // 2, 128)
        hi = t[:, 1].reshape(ITEM // 2, 128)
        packed = jnp.where(lane < 64, lo, pltpu.roll(hi, 64, axis=1))

        @pl.when(s < 2)
        def _():
            acc_row[half] = packed

        @pl.when(s >= 2)
        def _():
            part[s] = packed.astype(BF16)
            part_copy(s, dx, dc).start()

        return 0

    lax.fori_loop(0, len(ORDER), item, 0)

    grad = (acc_col[0:64] - acc_col[64:65] * cx[0:64].astype(F32)) * col_scale
    for p in range(8):
        block = grad[8 * p:8 * p + 8]
        back_out[p] = jnp.concatenate([block[:, :512], block[:, 512:]], axis=0).astype(BF16)

    def back_copy(d):
        return pltpu.make_async_remote_copy(
            src_ref=back_out.at[(row + d) % 8], dst_ref=back_in.at[row],
            send_sem=back_s.at[d], recv_sem=back_r.at[d], device_id=row_peer(d), device_id_type=MESH)

    back_copies = [back_copy(d) for d in range(1, 8)]
    for c in back_copies:
        c.start()
    back_in[row] = back_out[row]

    for s in range(2, len(ORDER)):
        part_copy(s, *ORDER[s][:2]).wait_recv()
    for h in range(2):
        total = acc_row[h]
        for s in range(2, len(ORDER)):
            if ORDER[s][2] == h:
                total += got[s].astype(F32)
        acc_row[h] = total
        y_out[2 * h:2 * h + 2] = total.reshape(2, 128, 128).astype(BF16)

    def yy_copy(d):
        return pltpu.make_async_remote_copy(
            src_ref=y_out.at[(y + d) % NY], dst_ref=y_in.at[d],
            send_sem=yy_s.at[d], recv_sem=yy_r.at[d], device_id=y_peer(d), device_id_type=MESH)

    yy_copies = [yy_copy(d) for d in range(1, NY)]
    for c in yy_copies:
        c.start()
    total = acc_row[y // 2, pl.ds(pl.multiple_of((y % 2) * 128, 128), 128)]
    for c, d in zip(yy_copies, range(1, NY)):
        c.wait_recv()
        total += y_in[d].astype(F32)
    z_out[...] = total.reshape(NZ, 16, 128).astype(BF16)

    def zz_copy(d):
        return pltpu.make_async_remote_copy(
            src_ref=z_out.at[(z + d) % NZ], dst_ref=z_in.at[d],
            send_sem=zz_s.at[d], recv_sem=zz_r.at[d], device_id=z_peer(d), device_id_type=MESH)

    zz_copies = [zz_copy(d) for d in range(1, NZ)]
    for c in zz_copies:
        c.start()
    total = z_out[z].astype(F32)
    for c, d in zip(zz_copies, range(1, NZ)):
        c.wait_recv()
        total += z_in[d].astype(F32)
    total = total * row_scale
    final = jnp.concatenate([total, pltpu.roll(total, 64, axis=1), jnp.zeros((96, 128), F32)], axis=0)
    out_rows[...] = final.T[0:64, 0:32]

    for c in back_copies:
        c.wait_recv()
    for p in range(8):
        block = back_in[p].astype(F32)
        out_cols[:, p * TILE:p * TILE + 512] = block[0:8]
        out_cols[:, p * TILE + 512:(p + 1) * TILE] = block[8:16]

    for c in z_copies + col_copies + y_copies + x_copies + back_copies + yy_copies + zz_copies:
        c.wait_send()
    for d in range(1, NX):
        core_copy(((x + d) % NX) * 2 + core, d).wait_send()
    for s in range(2, len(ORDER)):
        part_copy(s, *ORDER[s][:2]).wait_send()


def body(row_feats, row_alpha, row_solves, col_feats, col_alpha, col_weight, col_probes):
    row_size = lax.axis_size("row")
    col_size = lax.axis_size("col")
    window = row_alpha.shape[0] * row_size * col_size
    points = col_alpha.shape[0] * col_size
    dma = pltpu.SemaphoreType.DMA
    vmem = pl.BlockSpec(memory_space=pltpu.VMEM)
    items = len(ORDER)
    return pl.pallas_call(
        functools.partial(kernel, 1.0 / points**0.5, 1.0 / window**0.5),
        out_shape=(
            jax.ShapeDtypeStruct((FEAT, row_feats.shape[1]), F32),
            jax.ShapeDtypeStruct((FEAT // row_size, col_feats.shape[1]), F32),
        ),
        in_specs=[vmem] * 7,
        out_specs=(vmem, vmem),
        scratch_shapes=[
            pltpu.VMEM((2 * NX, NY, NZ, 32, 128), BF16),
            pltpu.VMEM((8, 16, 768), BF16),
            pltpu.VMEM((8, 16, 768), BF16),
            pltpu.VMEM((128, TILE), BF16),
            pltpu.VMEM((128, TILE), BF16),
            pltpu.VMEM((TILE, 128), BF16),
            pltpu.VMEM((80, TILE), F32),
            pltpu.VMEM((2, ITEM // 2, 128), F32),
            pltpu.VMEM((items, ITEM // 2, 128), BF16),
            pltpu.VMEM((items, ITEM // 2, 128), BF16),
            pltpu.VMEM((NY, 128, 128), BF16),
            pltpu.VMEM((NY, 128, 128), BF16),
            pltpu.VMEM((NZ, 16, 128), BF16),
            pltpu.VMEM((NZ, 16, 128), BF16),
            pltpu.VMEM((8, 16, 512), BF16),
            pltpu.VMEM((8, 16, 512), BF16),
            dma((8,)), dma((8,)), dma((NZ,)), dma((NZ,)), dma((NY,)), dma((NY,)),
            dma((NX,)), dma((2 * NX,)), dma((NX,)),
            dma((items,)), dma((items,)), dma((NY,)), dma((NY,)), dma((NZ,)), dma((NZ,)),
            dma((8,)), dma((8,)),
        ],
        compiler_params=pltpu.CompilerParams(
            collective_id=0, has_side_effects=True, vmem_limit_bytes=48 * 2**20),
        name="evidence_gradients",
    )(
        row_feats, row_alpha.reshape(1, -1), row_solves, col_feats,
        col_alpha.reshape(row_size, -1), col_weight.reshape(row_size, -1), col_probes,
    )


def solution(mesh):
    in_specs = (
        P(None, ("row", "col")),
        P(("row", "col")),
        P(None, ("row", "col")),
        P("row", "col"),
        P("col"),
        P("col"),
        P("row", "col"),
    )
    out_specs = (P(None, ("row", "col")), P("row", "col"))
    return jax.shard_map(body, mesh=mesh, in_specs=in_specs, out_specs=out_specs, check_vma=False)
```

time: 521 us -> 64.6 us (0.12)
  waiting for transfers between devices: 254 us -> 0 us
  blocking collectives: 186 us -> 0 us
  Pallas kernels: 0 us -> 58.5 us
  matrix products: 44.6 us -> 0 us
  between operations: 14.5 us -> 0.7 us
  local copies, waits for them, and re-layouts: 13.4 us -> 4.63 us
  other arithmetic: 7.81 us -> 0 us
    reduce_scatter x2 -> x0, waiting for transfers between devices: 252 us -> none  [the longest x1 137 us: body(): lax.psum_scatter(part_row, 'col', scatter_dimension=1, tiled=True)]
    all_gather x3 -> x0, blocking collectives: 123 us -> none  [the longest x1 49.2 us: body(): lax.all_gather(col_probes, 'row', axis=0, tiled=True)]
    unnamed x1 -> x0, blocking collectives: 63.3 us -> none
    pallas_call x0 -> x1, Pallas kernels: none -> 58.5 us  [body(): pl.pallas_call(functools.partial(kernel, 1.0 / points ** 0.5, 1.0 / windo...]
    dot_general x16 -> x0, matrix products: 44.6 us -> none  [the longest x4 17.8 us: tile_terms(): lax.dot_general(left, right, contract, preferred_element_type=jnp.float32)]
    while x25 -> x0, local copies, waits for them, and re-layouts: 8.91 us -> none
  transfers between devices with their start and end apart: 3 -> 0, of which waited for: 2 -> 0; matrix products, arithmetic and copies ran while one was open for 1% -> 0% of each run, Pallas kernels for 0% -> 0%
where the time goes in v1:
time: 64.6 us; the launch traced here: 63.9 us
  Pallas kernels  58.5 us (91%)
  local copies, waits for them, and re-layouts  4.63 us (7%)
  between operations  0.7 us (1%)
    pallas_call x1, Pallas kernels, body(): pl.pallas_call(functools.partial(kernel, 1.0 / points ** 0.5, 1.0 / windo...  58.5 us
    unnamed x10, local copies, waits for them, and re-layouts  2.44 us

profile of v1, /device:TPU:2, one launch (start us, length us, event | category | flops | bytes accessed | tf_op | source)
XLA Modules:
  0.0 63.9 jit_solution(8985224850578518885)
XLA Ops:
  0.6 0.0 copy-start.1
  0.6 0.8 %copy.9.rf_ref = bf16[64,32]{1,0:T(8,128)(2,1)S(1)} copy(bf16[64,32]{0,1:T(8,128)(2,1)} %param.7) | data formatting | bytes 8192 | tf_op args[0]
  1.5 0.7 %reshape.14.ca_ref = bf16[8,1024]{1,0:T(8,128)(2,1)S(1)} reshape(bf16[8192]{0:T(1024)(128)(2,1)} %param.11) | data formatting | bytes 32768 | tf_op jit(solution)/shard_map/reshape | solution.py:325
  2.2 0.0 copy-start.2
  2.2 0.0 copy-start.3
  2.2 0.8 %reshape.15.cw_ref = f32[8,1024]{1,0:T(8,128)S(1)} reshape(f32[8192]{0:T(1024)} %param.12) | data formatting | bytes 65536 | tf_op jit(solution)/shard_map/reshape | solution.py:325
  3.0 0.0 copy-done.1
  3.0 0.0 copy-done.2
  3.0 0.0 copy-done.3
  3.0 0.0 copy-start
  3.0 0.9 %copy-done = bf16[8,8192]{1,0:T(8,128)(2,1)S(1)} copy-done((bf16[8,8192]{1,0:T(8,128)(2,1)S(1)}, bf16[8,8192]{1,0:T(8,128)(2,1)}, u32[]{:S(2)}) %copy-start) | copy-done | bytes 131096
  3.9 58.5 %evidence_gradients.1 = (f32[64,32]{1,0:T(8,128)S(1)}, f32[8,8192]{1,0:T(8,128)S(1)}) custom-call(bf16[64,32]{1,0:T(8,128)(2,1)S(1)} %copy.9.rf_ref, bf16[1,32]{1,0:T(2,128)(2,1)S(1)} %bitcast.1, bf16[32,32]{1,0:T(8,128)(2,1)S(1)} %copy-done.2, bf16[8,8192]{1,0:T(8,128)(2,1)S(1)} %copy-done, bf16[8,1024]{1,0:T(8,128)(2,1)S(1)} %reshape.14.ca_ref, ...), custom_call_target="tpu_custom_call" | custom-call | tf_op jit(solution)/shard_map/evidence_gradients/pallas_call | solution.py:290
  62.5 0.7 %copy.10 = f32[64,32]{0,1:T(8,128)} copy(f32[64,32]{1,0:T(8,128)S(1)} %get-tuple-element.2) | data formatting | bytes 16384 | tf_op jit(solution)/shard_map/evidence_gradients/pallas_call | solution.py:290
  63.2 0.7 %copy.12 = f32[8,8192]{1,0:T(8,128)} copy(f32[8,8192]{1,0:T(8,128)S(1)} %get-tuple-element.7) | data formatting | bytes 524288
Async XLA Ops:
  0.6 2.4 %copy-start.1 = (bf16[4,8192]{1,0:T(4,128)(2,1)S(1)}, bf16[4,8192]{1,0:T(4,128)(2,1)}, u32[]{:S(2)}) copy-start(bf16[4,8192]{1,0:T(4,128)(2,1)} %cp_ref.1) | copy-start | bytes 196612
  2.2 0.8 %copy-start.2 = (bf16[32,32]{1,0:T(8,128)(2,1)S(1)}, bf16[32,32]{1,0:T(8,128)(2,1)}, u32[]{:S(2)}) copy-start(bf16[32,32]{1,0:T(8,128)(2,1)} %rs_ref.1) | copy-start | bytes 6148
  2.2 0.8 %copy-start.3 = (bf16[32]{0:T(256)(128)(2,1)S(1)}, bf16[32]{0:T(256)(128)(2,1)}, u32[]{:S(2)}) copy-start(bf16[32]{0:T(256)(128)(2,1)} %param.8) | copy-start | bytes 196
  3.0 0.9 %copy-start = (bf16[8,8192]{1,0:T(8,128)(2,1)S(1)}, bf16[8,8192]{1,0:T(8,128)(2,1)}, u32[]{:S(2)}) copy-start(bf16[8,8192]{1,0:T(8,128)(2,1)} %cf_ref.1) | copy-start | bytes 393220

commit v2 on v1

v2 whole, which is shorter than its diff:
```python
import functools

import jax
import jax.numpy as jnp
from jax import lax
from jax.experimental import pallas as pl
from jax.experimental.pallas import tpu as pltpu
from jax.sharding import PartitionSpec as P

MESH = pl.DeviceIdType.MESH
F32 = jnp.float32
BF16 = jnp.bfloat16

FEAT = 64
PROBES = 32
NX, NY, NZ = 4, 4, 8
TILE = 1024
ITEM = 512
HALF = 16

ORDER = (
    ((0, 0), (1, 0), (1, 1), (3, 0), (3, 1), (2, 0), (2, 1), (0, 1)),
    ((0, 1), (1, 0), (1, 1), (3, 0), (3, 1), (2, 0), (2, 1), (0, 0)),
)
ITEMS = 16
F8 = jnp.float8_e4m3fn
UP = 512.0
LOG2E = 1.4426950408889634


def look(values, at):
    out = jnp.int32(values[0])
    for k, v in enumerate(values[1:], 1):
        out = jnp.where(at == k, jnp.int32(v), out)
    return out


def lookup(s, k):
    flat = [ORDER[i % 2][i // 2][k] for i in range(ITEMS)]
    return look(flat, s)


def split8(v):
    hi = v.astype(F8).astype(F32)
    return hi, (v - hi).astype(F8).astype(F32)


def parts3(v):
    hi = v.astype(BF16).astype(F32)
    mid = (v - hi).astype(BF16).astype(F32)
    return hi, mid, v - hi - mid


def kernel(
    row_scale, col_scale,
    rf_hbm, ra_hbm, rs_hbm, cf_hbm, ca_hbm, cw_hbm, cp_hbm,
    out_rows, out_cols,
    rf_ref, ra_ref, rs_ref, cf_ref, ca_ref, cw_ref, cp_ref, in_s,
    zbuf, rows, send_cols, recv_cols, relay, cx, cf8, cb, cr, xct, small, acc_col,
    keep, core_out, core_in, axis_out, axis_in,
    mid_out, mid_in, z_out, z_in, back_out, back_in, back_relay,
    col_s, col_r, z_s, z_r, m_s, m_r, g_s, g_r, f_s,
    core_s, core_r, axis_s, axis_r, mm_s, mm_r, zz_s, zz_r, back_s, back_r,
):
    row = lax.axis_index("row")
    col = lax.axis_index("col")
    y, core = row % 4, col % 2
    x, z = col // 8, (row // 4) * 4 + (col // 2) % 4

    def at(px, py, pz, pc):
        return {"row": (pz // 4) * 4 + py, "col": (px * 4 + pz % 4) * 2 + pc}

    def z_peer(d):
        return at(x, y, (z + d) % NZ, core)

    def axis_peer(t, d):
        return at((x + jnp.where(t == 0, d, 0)) % NX, (y + jnp.where(t == 1, d, 0)) % NY, z, core)

    sibling = at(x, y, z, 1 - core)
    far = (row + 4) % 8

    def row_of(d, other):
        return ((row // 4 + other) % 2) * 4 + (y + d) % 4

    def exchange(out, into, through, send, recv):
        def over_z(d):
            return pltpu.make_async_remote_copy(
                src_ref=out.at[row_of(d, 1)], dst_ref=through.at[d] if d else into.at[row],
                send_sem=send.at[0, d], recv_sem=recv.at[0, d], device_id=z_peer(4), device_id_type=MESH)

        def over_y(d):
            return pltpu.make_async_remote_copy(
                src_ref=out.at[row_of(d, 0)], dst_ref=into.at[row],
                send_sem=send.at[1, d], recv_sem=recv.at[1, d], device_id=axis_peer(1, d), device_id_type=MESH)

        def onward(d):
            return pltpu.make_async_remote_copy(
                src_ref=through.at[d], dst_ref=into.at[far],
                send_sem=send.at[2, d], recv_sem=recv.at[2, d], device_id=axis_peer(1, d), device_id_type=MESH)

        first = [over_z(d) for d in (2, 1, 3, 0)]
        second = [over_y(d) for d in (2, 1, 3)]
        third = [onward(d) for d in (2, 1, 3)]

        def start():
            for c in first + second:
                c.start()
            into[row] = out[row]

        def forward():
            for a, b in zip(first, third):
                a.wait_recv()
                b.start()

        def finish():
            for c in second + [first[3]] + third:
                c.wait_recv()

        def sent():
            for c in first + second + third:
                c.wait_send()

        return start, forward, finish, sent

    loads = [
        pltpu.make_async_copy(src, dst, in_s.at[k])
        for k, (src, dst) in enumerate((
            (rf_hbm, rf_ref), (ra_hbm, ra_ref), (rs_hbm, rs_ref), (cf_hbm, cf_ref),
            (cp_hbm, cp_ref), (ca_hbm, ca_ref), (cw_hbm, cw_ref)))
    ]
    for c in loads:
        c.start()

    barrier = pltpu.get_barrier_semaphore()
    peers = [z_peer(d) for d in range(1, NZ)] + [sibling]
    peers += [axis_peer(t, d) for t in range(2) for d in range(1, 4)]
    for peer in peers:
        pl.semaphore_signal(barrier, inc=1, device_id=peer, device_id_type=MESH)

    for c in loads[:3]:
        c.wait()
    n = 2 * HALF
    rf = rf_ref[...].astype(F32)
    sq = -0.5 * jnp.sum(rf * rf, axis=1, keepdims=True)
    at8 = lax.broadcasted_iota(jnp.int32, (8, n), 0)
    side = jnp.concatenate(
        [jnp.zeros((64, n), F32), jnp.where(at8 == 6, ra_ref[...].astype(F32), 0.0),
         rs_ref[...].astype(F32), jnp.zeros((24, n), F32)], axis=0)
    side = jnp.concatenate([side, jnp.zeros((128, 128 - n), F32)], axis=1).T[:n]
    lane = lax.broadcasted_iota(jnp.int32, (n, 128), 1)
    mine = side + jnp.concatenate([rf, jnp.zeros((n, 64), F32)], axis=1)
    mine = jnp.where(jnp.logical_and(lane >= 64, lane < 67), 1.0, mine)
    for k, v in enumerate(parts3(sq)):
        mine = jnp.where(lane == 67 + k, v, mine)
    zbuf[z] = mine.astype(BF16)

    for c in loads[3:5]:
        c.wait()
    for p in range(8):
        feats = cf_ref[:, p * TILE:(p + 1) * TILE].astype(F32)
        probes = cp_ref[:, p * TILE:(p + 1) * TILE].astype(F32)
        left = jnp.concatenate([feats[:, :512], feats[:, 512:]], axis=0)
        right = jnp.concatenate([probes[:, q * 256:(q + 1) * 256] for q in range(4)], axis=0)
        send_cols[p] = jnp.concatenate([left, right], axis=1).astype(BF16)

    pl.semaphore_wait(barrier, len(peers))

    def z_copy(d):
        return pltpu.make_async_remote_copy(
            src_ref=zbuf.at[z], dst_ref=zbuf.at[z],
            send_sem=z_s.at[d], recv_sem=z_r.at[d], device_id=z_peer(d), device_id_type=MESH)

    own = (x * 2 + core, y * 2 + core)
    place = (y, x)

    def m_copy(t, d):
        return pltpu.make_async_remote_copy(
            src_ref=rows.at[t, own[t], place[t]], dst_ref=rows.at[t, own[t], place[t]],
            send_sem=m_s.at[t, d], recv_sem=m_r.at[t, d], device_id=axis_peer(1 - t, d), device_id_type=MESH)

    def g_copy(t, g, peer, send_sem):
        return pltpu.make_async_remote_copy(
            src_ref=rows.at[t, g], dst_ref=rows.at[t, g],
            send_sem=send_sem, recv_sem=g_r.at[t, g], device_id=peer, device_id_type=MESH)

    def group(t, d, dc):
        return jnp.where(t == 0, (x + d) % NX, (y + d) % NY) * 2 + (core + dc) % 2

    def axis_copy(t, d):
        return g_copy(t, group(t, 0, 0), axis_peer(t, d), g_s.at[t, d])

    def sibling_copy(t, d):
        return g_copy(t, group(t, d, 0), sibling, f_s.at[t, d])

    z_copies = [z_copy(d) for d in range(1, NZ)]
    for c in z_copies:
        c.start()
    col_start, col_forward, col_finish, col_sent = exchange(send_cols, recv_cols, relay, col_s, col_r)
    col_start()
    for c in z_copies:
        c.wait_recv()
    m_copies = []
    for t in range(2):
        rows[t, own[t], place[t]] = zbuf[:, t * HALF:(t + 1) * HALF]
        m_copies.append([m_copy(t, d) for d in range(1, 4)])
        for c in m_copies[t]:
            c.start()
    col_forward()
    for t in range(2):
        for c in m_copies[t]:
            c.wait_recv()
        sibling_copy(t, 0).start()
        axis_copy(t, 1).start()
        axis_copy(t, 3).start()
    col_finish()

    feats = jnp.concatenate(
        [jnp.concatenate([recv_cols[p, :, 0:512].astype(F32)[8 * h:8 * h + 8] for h in range(2)], axis=1)
         for p in range(8)], axis=0)
    probes = []
    for p in range(8):
        block = recv_cols[p, :, 512:768].astype(F32)
        probes.append(jnp.concatenate([block[4 * q:4 * q + 4] for q in range(4)], axis=1))
    probes = jnp.concatenate(probes, axis=0)
    for c in loads[5:]:
        c.wait()
    eight = pl.ds(pl.multiple_of(row * 8, 8), 8)
    weight = cw_ref[eight, :]
    small[...] = ca_ref[...].astype(F32)
    alpha = small[eight, :]
    weight = jnp.concatenate([weight[k:k + 1] for k in range(8)], axis=1)
    alpha = jnp.concatenate([alpha[k:k + 1] for k in range(8)], axis=1)
    cb[...] = (-0.5 * LOG2E) * jnp.sum(feats * feats, axis=0, keepdims=True)
    cx[...] = feats.astype(BF16)
    hi, lo = split8(feats * UP)
    cf8[...] = jnp.concatenate([hi, lo, lo, hi], axis=0).astype(F8)
    at8 = lax.broadcasted_iota(jnp.int32, (8, TILE), 0)
    cr[...] = jnp.concatenate(
        [jnp.zeros((64, TILE), F32), jnp.where(at8 == 6, 0.5 * alpha, 0.0), (-0.5 / PROBES) * weight * probes,
         jnp.zeros((24, TILE), F32)], axis=0).astype(BF16)
    xct[...] = jnp.concatenate(
        [feats, jnp.where(at8 == 0, 1.0, 0.0), jnp.zeros((56, TILE), F32)], axis=0).T.astype(BF16)

    acc_col[...] = jnp.zeros_like(acc_col)
    lane = lax.broadcasted_iota(jnp.int32, (ITEM, 128), 1)

    def core_copy(t, d):
        return pltpu.make_async_remote_copy(
            src_ref=core_out.at[t, d], dst_ref=core_in.at[t, d],
            send_sem=core_s.at[t, d], recv_sem=core_r.at[t, d], device_id=sibling, device_id_type=MESH)

    def part_copy(t, d):
        return pltpu.make_async_remote_copy(
            src_ref=axis_out.at[t, d], dst_ref=axis_in.at[t, d],
            send_sem=axis_s.at[t, d], recv_sem=axis_r.at[t, d], device_id=axis_peer(t, d), device_id_type=MESH)

    def item(s, _):
        t = s % 2
        d, dc = lookup(s, 0), lookup(s, 1)
        borrowed = jnp.logical_and(s != 0, s != ITEMS - 1)
        g = group(t, d, dc)

        @pl.when(borrowed)
        def _():
            g_copy(t, g, sibling, f_s.at[t, 0]).wait_recv()

        @pl.when(jnp.logical_and(dc == 0, borrowed))
        def _():
            sibling_copy(t, d).start()

        @pl.when(jnp.logical_and(d == 1, dc == 0))
        def _():
            axis_copy(t, 2).start()

        r = rows[t, g].reshape(ITEM, 128)
        wide = r.astype(F32)
        hi, lo = split8(jnp.where(lane < 64, wide * UP, 0.0))
        both = jnp.where(lane < 64, hi, pltpu.roll(lo, 64, axis=1)).astype(F8)
        squares = jnp.where(jnp.logical_and(lane >= 67, lane < 70), wide * LOG2E, 0.0)
        squares = jnp.sum(squares, axis=1, keepdims=True)
        cross = jnp.dot(jnp.concatenate([both, both], axis=1), cf8[...], preferred_element_type=F32)
        weights = jnp.dot(r, cr[...], preferred_element_type=F32)
        prod = (weights * jnp.exp2(cross * (LOG2E / UP**2) + cb[...] + squares)).astype(BF16)
        out = jnp.dot(prod, xct[...], preferred_element_type=F32)
        acc_col[...] += jnp.dot(r.T[0:80], prod, preferred_element_type=F32)
        out = out - out[:, 64:65] * wide
        out = out.reshape(ITEM // HALF, 2, 8, 128)
        lo = out[:, 0].reshape(ITEM // 2, 128)
        hi = out[:, 1].reshape(ITEM // 2, 128)
        packed = jnp.where(lane[:ITEM // 2] < 64, lo, pltpu.roll(hi, 64, axis=1))

        @pl.when(dc == 0)
        def _():
            keep[t, d] = packed

        @pl.when(dc == 1)
        def _():
            core_out[t, d] = packed.astype(BF16)
            core_copy(t, d).start()

        before = 1 - t
        bd, bdc = lookup(s - 1, 0), lookup(s - 1, 1)

        @pl.when(jnp.logical_and(bdc == 1, bd != 0))
        def _():
            core_copy(before, bd).wait_recv()
            axis_out[before, bd] = (keep[before, bd] + core_in[before, bd].astype(F32)).astype(BF16)
            part_copy(before, bd).start()

        return 0

    lax.fori_loop(0, ITEMS, item, 0)

    grad = (acc_col[0:64] - acc_col[64:65] * cx[0:64].astype(F32)) * col_scale
    for p in range(8):
        block = grad[8 * p:8 * p + 8]
        back_out[p] = jnp.concatenate([block[:, :512], block[:, 512:]], axis=0).astype(BF16)

    back_start, back_forward, back_finish, back_sent = exchange(back_out, back_in, back_relay, back_s, back_r)
    back_start()

    def mm_copy(t, d):
        return pltpu.make_async_remote_copy(
            src_ref=mid_out.at[t, (place[t] + d) % 4], dst_ref=mid_in.at[t, d],
            send_sem=mm_s.at[t, d], recv_sem=mm_r.at[t, d], device_id=axis_peer(1 - t, d), device_id_type=MESH)

    mm_copies = []
    for t in range(2):
        core_copy(t, 0).wait_recv()
        total = keep[t, 0] + core_in[t, 0].astype(F32)
        for d in range(1, 4):
            part_copy(t, d).wait_recv()
            total += axis_in[t, d].astype(F32)
        keep[t, 0] = total
        mid_out[t] = total.reshape(4, 64, 128).astype(BF16)
        mm_copies.append([mm_copy(t, d) for d in range(1, 4)])
        for c in mm_copies[t]:
            c.start()
    back_forward()
    halves = []
    for t in range(2):
        total = keep[t, 0, pl.ds(pl.multiple_of(place[t] * 64, 64), 64), :]
        for c, d in zip(mm_copies[t], range(1, 4)):
            c.wait_recv()
            total += mid_in[t, d].astype(F32)
        halves.append(total.reshape(NZ, 8, 128))
    z_out[...] = jnp.concatenate(halves, axis=1).astype(BF16)

    def zz_copy(d):
        return pltpu.make_async_remote_copy(
            src_ref=z_out.at[(z + d) % NZ], dst_ref=z_in.at[d],
            send_sem=zz_s.at[d], recv_sem=zz_r.at[d], device_id=z_peer(d), device_id_type=MESH)

    zz_copies = [zz_copy(d) for d in range(1, NZ)]
    for c in zz_copies:
        c.start()
    total = z_out[z].astype(F32)
    for c, d in zip(zz_copies, range(1, NZ)):
        c.wait_recv()
        total += z_in[d].astype(F32)
    total = total * row_scale
    moved = pltpu.roll(total, 64, axis=1)
    final = jnp.concatenate([total[0:8], moved[0:8], total[8:16], moved[8:16]], axis=0)
    out_rows[...] = final[:, 0:64]

    back_finish()
    for p in range(8):
        block = back_in[p].astype(F32)
        out_cols[:, p * TILE:p * TILE + 512] = block[0:8]
        out_cols[:, p * TILE + 512:(p + 1) * TILE] = block[8:16]

    col_sent()
    back_sent()
    for c in z_copies + m_copies[0] + m_copies[1] + mm_copies[0] + mm_copies[1] + zz_copies:
        c.wait_send()
    for t in range(2):
        for d in range(4):
            sibling_copy(t, d).wait_send()
            core_copy(t, d).wait_send()
            if d:
                axis_copy(t, d).wait_send()
                part_copy(t, d).wait_send()


def body(row_feats, row_alpha, row_solves, col_feats, col_alpha, col_weight, col_probes):
    row_size = lax.axis_size("row")
    col_size = lax.axis_size("col")
    own_rows = row_alpha.shape[0]
    own_cols = col_alpha.shape[0]
    window = own_rows * row_size * col_size
    points = own_cols * col_size
    dma = pltpu.SemaphoreType.DMA
    vmem = pl.BlockSpec(memory_space=pltpu.VMEM)
    hbm = pl.BlockSpec(memory_space=pltpu.HBM)
    args = (
        row_feats.T, row_alpha.reshape(1, -1), row_solves, col_feats,
        col_alpha.reshape(-1, 128), col_weight.reshape(-1, 128), col_probes,
    )
    half = ITEM // 2
    grad_rows, grad_cols = pl.pallas_call(
        functools.partial(kernel, 1.0 / points**0.5, 1.0 / window**0.5),
        out_shape=(
            jax.ShapeDtypeStruct((own_rows, FEAT), F32),
            jax.ShapeDtypeStruct((FEAT // row_size, own_cols), F32),
        ),
        in_specs=[hbm] * 7,
        out_specs=(vmem, vmem),
        scratch_shapes=[
            *[pltpu.VMEM(a.shape, a.dtype) for a in args],
            dma((7,)),
            pltpu.VMEM((NZ, 2 * HALF, 128), BF16),
            pltpu.VMEM((2, 8, 4, NZ, HALF, 128), BF16),
            pltpu.VMEM((8, 16, 768), BF16),
            pltpu.VMEM((8, 16, 768), BF16),
            pltpu.VMEM((4, 16, 768), BF16),
            pltpu.VMEM((FEAT, TILE), BF16),
            pltpu.VMEM((4 * FEAT, TILE), F8),
            pltpu.VMEM((1, TILE), F32),
            pltpu.VMEM((128, TILE), BF16),
            pltpu.VMEM((TILE, 128), BF16),
            pltpu.VMEM((own_cols // 128, 128), F32),
            pltpu.VMEM((80, TILE), F32),
            pltpu.VMEM((2, 4, half, 128), F32),
            *[pltpu.VMEM((2, 4, half, 128), BF16)] * 4,
            *[pltpu.VMEM((2, 4, half // 4, 128), BF16)] * 2,
            *[pltpu.VMEM((NZ, 16, 128), BF16)] * 2,
            *[pltpu.VMEM((8, 16, 512), BF16)] * 2,
            pltpu.VMEM((4, 16, 512), BF16),
            dma((3, 4)), dma((3, 4)), dma((NZ,)), dma((NZ,)), dma((2, 4)), dma((2, 4)),
            dma((2, 4)), dma((2, 8)), dma((2, 4)),
            *[dma((2, 4))] * 6,
            dma((NZ,)), dma((NZ,)), dma((3, 4)), dma((3, 4)),
        ],
        compiler_params=pltpu.CompilerParams(
            collective_id=0, has_side_effects=True, vmem_limit_bytes=63 * 2**20),
        name="evidence_gradients",
    )(*args)
    return grad_rows.T, grad_cols


def solution(mesh):
    in_specs = (
        P(None, ("row", "col")),
        P(("row", "col")),
        P(None, ("row", "col")),
        P("row", "col"),
        P("col"),
        P("col"),
        P("row", "col"),
    )
    out_specs = (P(None, ("row", "col")), P("row", "col"))
    return jax.shard_map(body, mesh=mesh, in_specs=in_specs, out_specs=out_specs, check_vma=False)
```

time: 64.6 us -> 60.6 us (0.938)
  Pallas kernels: 58.5 us -> 56.8 us
  local copies, waits for them, and re-layouts: 4.63 us -> 2.99 us
    pallas_call x1, Pallas kernels: 58.5 us -> 56.8 us  [body(): pl.pallas_call(functools.partial(kernel, 1.0 / points ** 0.5, 1.0 / windo...]
    reshape x2 -> x0, local copies, waits for them, and re-layouts: 1.52 us -> none  [the longest x1 0.78 us: body(): col_weight.reshape(row_size, -1)]
    pallas_call x1 -> x0, local copies, waits for them, and re-layouts: 0.68 us -> none  [body(): pl.pallas_call(functools.partial(kernel, 1.0 / points ** 0.5, 1.0 / windo...]
    unnamed x10 -> x2, local copies, waits for them, and re-layouts: 2.44 us -> 2.99 us
where the time goes in v2:
time: 60.6 us; the launch traced here: 60.4 us
  Pallas kernels  56.8 us (94%)
  local copies, waits for them, and re-layouts  2.99 us (5%)
  between operations  0.64 us (1%)
    pallas_call x1, Pallas kernels, body(): pl.pallas_call(functools.partial(kernel, 1.0 / points ** 0.5, 1.0 / windo...  56.8 us
    unnamed x2, local copies, waits for them, and re-layouts  2.99 us

profile of v2, /device:TPU:2, one launch (start us, length us, event | category | flops | bytes accessed | tf_op | source)
XLA Modules:
  0.0 60.4 jit_solution(5004377234478408695)
XLA Ops:
  0.6 56.8 %evidence_gradients.1 = (f32[32,64]{1,0:T(8,128)}, f32[8,8192]{1,0:T(8,128)}) custom-call(bf16[32,64]{1,0:T(8,128)(2,1)} %bitcast.8, bf16[1,32]{1,0:T(2,128)(2,1)} %bitcast.9, bf16[32,32]{1,0:T(8,128)(2,1)} %rs_hbm.1, bf16[8,8192]{1,0:T(8,128)(2,1)} %cf_hbm.1, bf16[64,128]{1,0:T(8,128)(2,1)} %bitcast.6, f32[64,128]{1,0:T(8,128)} %bitcast.5, ...), custom_call_target="tpu_custom_call" | custom-call | tf_op jit(solution)/shard_map/evidence_gradients/pallas_call | solution.py:400
  57.4 1.3 %copy.11 = f32[64,32]{0,1:T(8,128)} copy(f32[64,32]{0,1:T(8,128)} %bitcast.7) | data formatting | bytes 16384
  58.7 1.7 %copy.12 = f32[8,8192]{1,0:T(8,128)} copy(f32[8,8192]{1,0:T(8,128)} %get-tuple-element.9) | data formatting | bytes 524288

commit v3 on v2

--- a/solution.py
+++ b/solution.py
@@ -18,14 +18,9 @@
 ITEM = 512
 HALF = 16
 
-ORDER = (
-    ((0, 0), (1, 0), (1, 1), (3, 0), (3, 1), (2, 0), (2, 1), (0, 1)),
-    ((0, 1), (1, 0), (1, 1), (3, 0), (3, 1), (2, 0), (2, 1), (0, 0)),
-)
-ITEMS = 16
-F8 = jnp.float8_e4m3fn
-UP = 512.0
-LOG2E = 1.4426950408889634
+ORDER = ((0, 1), (1, 0), (1, 1), (3, 1), (3, 0), (2, 1), (2, 0), (0, 0))
+PASS_ON = (0, 1, 3, 0, 2, 0, 0, 0)
+ADD_UP = (0, 0, 0, 1, 3, 0, 2, 0)
 
 
 def look(values, at):
@@ -35,16 +30,6 @@
     return out
 
 
-def lookup(s, k):
-    flat = [ORDER[i % 2][i // 2][k] for i in range(ITEMS)]
-    return look(flat, s)
-
-
-def split8(v):
-    hi = v.astype(F8).astype(F32)
-    return hi, (v - hi).astype(F8).astype(F32)
-
-
 def parts3(v):
     hi = v.astype(BF16).astype(F32)
     mid = (v - hi).astype(BF16).astype(F32)
@@ -56,7 +41,7 @@
     rf_hbm, ra_hbm, rs_hbm, cf_hbm, ca_hbm, cw_hbm, cp_hbm,
     out_rows, out_cols,
     rf_ref, ra_ref, rs_ref, cf_ref, ca_ref, cw_ref, cp_ref, in_s,
-    zbuf, rows, send_cols, recv_cols, relay, cx, cf8, cb, cr, xct, small, acc_col,
+    zbuf, rows, send_cols, recv_cols, relay, cx, cr, xct, small, acc_col,
     keep, core_out, core_in, axis_out, axis_in,
     mid_out, mid_in, z_out, z_in, back_out, back_in, back_relay,
     col_s, col_r, z_s, z_r, m_s, m_r, g_s, g_r, f_s,
@@ -157,11 +142,23 @@
     for c in loads[3:5]:
         c.wait()
     for p in range(8):
-        feats = cf_ref[:, p * TILE:(p + 1) * TILE].astype(F32)
-        probes = cp_ref[:, p * TILE:(p + 1) * TILE].astype(F32)
+        span = slice(p * TILE, (p + 1) * TILE)
+        feats = cf_ref[:, span].astype(F32)
+        probes = cp_ref[:, span].astype(F32)
         left = jnp.concatenate([feats[:, :512], feats[:, 512:]], axis=0)
         right = jnp.concatenate([probes[:, q * 256:(q + 1) * 256] for q in range(4)], axis=0)
         send_cols[p] = jnp.concatenate([left, right], axis=1).astype(BF16)
+
+    for c in loads[5:]:
+        c.wait()
+    eight = pl.ds(pl.multiple_of(row * 8, 8), 8)
+    weight = cw_ref[eight, :]
+    small[...] = ca_ref[...].astype(F32)
+    alpha = small[eight, :]
+    weight = jnp.concatenate([weight[k:k + 1] for k in range(8)], axis=1) * (-0.5 / PROBES)
+    alpha = jnp.concatenate([alpha[k:k + 1] for k in range(8)], axis=1) * 0.5
+    xct[:, 128:] = jnp.ones((TILE, 128), BF16)
+    acc_col[...] = jnp.zeros_like(acc_col)
 
     pl.semaphore_wait(barrier, len(peers))
 
@@ -215,34 +212,46 @@
     col_finish()
 
     feats = jnp.concatenate(
-        [jnp.concatenate([recv_cols[p, :, 0:512].astype(F32)[8 * h:8 * h + 8] for h in range(2)], axis=1)
+        [jnp.concatenate([recv_cols[p, :, 0:512].astype(F32)[8 * k:8 * k + 8] for k in range(2)], axis=1)
          for p in range(8)], axis=0)
     probes = []
     for p in range(8):
         block = recv_cols[p, :, 512:768].astype(F32)
         probes.append(jnp.concatenate([block[4 * q:4 * q + 4] for q in range(4)], axis=1))
     probes = jnp.concatenate(probes, axis=0)
-    for c in loads[5:]:
-        c.wait()
-    eight = pl.ds(pl.multiple_of(row * 8, 8), 8)
-    weight = cw_ref[eight, :]
-    small[...] = ca_ref[...].astype(F32)
-    alpha = small[eight, :]
-    weight = jnp.concatenate([weight[k:k + 1] for k in range(8)], axis=1)
-    alpha = jnp.concatenate([alpha[k:k + 1] for k in range(8)], axis=1)
-    cb[...] = (-0.5 * LOG2E) * jnp.sum(feats * feats, axis=0, keepdims=True)
-    cx[...] = feats.astype(BF16)
-    hi, lo = split8(feats * UP)
-    cf8[...] = jnp.concatenate([hi, lo, lo, hi], axis=0).astype(F8)
+    sq = parts3(-0.5 * jnp.sum(feats * feats, axis=0, keepdims=True))
     at8 = lax.broadcasted_iota(jnp.int32, (8, TILE), 0)
+    side = jnp.where(at8 < 6, 1.0, 0.0)
+    for k, v in enumerate(sq):
+        side = jnp.where(at8 == k, v, side)
+    cx[...] = jnp.concatenate([feats, side, jnp.zeros((56, TILE), F32)], axis=0).astype(BF16)
     cr[...] = jnp.concatenate(
-        [jnp.zeros((64, TILE), F32), jnp.where(at8 == 6, 0.5 * alpha, 0.0), (-0.5 / PROBES) * weight * probes,
+        [jnp.zeros((64, TILE), F32), jnp.where(at8 == 6, alpha, 0.0), weight * probes,
          jnp.zeros((24, TILE), F32)], axis=0).astype(BF16)
-    xct[...] = jnp.concatenate(
-        [feats, jnp.where(at8 == 0, 1.0, 0.0), jnp.zeros((56, TILE), F32)], axis=0).T.astype(BF16)
-
-    acc_col[...] = jnp.zeros_like(acc_col)
-    lane = lax.broadcasted_iota(jnp.int32, (ITEM, 128), 1)
+    xct[:, 0:128] = jnp.concatenate([feats, feats], axis=0).T.astype(BF16)
+
+    low = lax.broadcasted_iota(jnp.int32, (ITEM, 128), 1) < 64
+
+    def groups(g0, g1):
+        return jnp.concatenate([rows[0, g0].reshape(ITEM, 128), rows[1, g1].reshape(ITEM, 128)], axis=0)
+
+    def products(r):
+        cross = jnp.dot(r, cx[...], preferred_element_type=F32)
+        weights = jnp.dot(r, cr[...], preferred_element_type=F32)
+        prod = (weights * jnp.exp(cross)).astype(BF16)
+        out = jnp.dot(prod, xct[...], preferred_element_type=F32)
+        acc_col[...] += jnp.dot(r.T[0:80], prod, preferred_element_type=F32)
+        return out
+
+    def pack(out, r):
+        def pick(v, k):
+            return v.reshape(2 * ITEM // HALF, 2, 8, 128)[:, k].reshape(ITEM, 128)
+
+        wide = r.astype(F32)
+        feats = jnp.where(low, pick(wide, 0), pltpu.roll(pick(wide, 1), 64, axis=1))
+        toward, total = out[:, :128], out[:, 128:]
+        return (jnp.where(low, pick(toward, 0), pick(toward, 1))
+                - jnp.where(low, pick(total, 0), pick(total, 1)) * feats)
 
     def core_copy(t, d):
         return pltpu.make_async_remote_copy(
@@ -254,68 +263,57 @@
             src_ref=axis_out.at[t, d], dst_ref=axis_in.at[t, d],
             send_sem=axis_s.at[t, d], recv_sem=axis_r.at[t, d], device_id=axis_peer(t, d), device_id_type=MESH)
 
-    def item(s, _):
-        t = s % 2
-        d, dc = lookup(s, 0), lookup(s, 1)
-        borrowed = jnp.logical_and(s != 0, s != ITEMS - 1)
-        g = group(t, d, dc)
-
-        @pl.when(borrowed)
-        def _():
-            g_copy(t, g, sibling, f_s.at[t, 0]).wait_recv()
-
-        @pl.when(jnp.logical_and(dc == 0, borrowed))
-        def _():
-            sibling_copy(t, d).start()
-
-        @pl.when(jnp.logical_and(d == 1, dc == 0))
-        def _():
-            axis_copy(t, 2).start()
-
-        r = rows[t, g].reshape(ITEM, 128)
-        wide = r.astype(F32)
-        hi, lo = split8(jnp.where(lane < 64, wide * UP, 0.0))
-        both = jnp.where(lane < 64, hi, pltpu.roll(lo, 64, axis=1)).astype(F8)
-        squares = jnp.where(jnp.logical_and(lane >= 67, lane < 70), wide * LOG2E, 0.0)
-        squares = jnp.sum(squares, axis=1, keepdims=True)
-        cross = jnp.dot(jnp.concatenate([both, both], axis=1), cf8[...], preferred_element_type=F32)
-        weights = jnp.dot(r, cr[...], preferred_element_type=F32)
-        prod = (weights * jnp.exp2(cross * (LOG2E / UP**2) + cb[...] + squares)).astype(BF16)
-        out = jnp.dot(prod, xct[...], preferred_element_type=F32)
-        acc_col[...] += jnp.dot(r.T[0:80], prod, preferred_element_type=F32)
-        out = out - out[:, 64:65] * wide
-        out = out.reshape(ITEM // HALF, 2, 8, 128)
-        lo = out[:, 0].reshape(ITEM // 2, 128)
-        hi = out[:, 1].reshape(ITEM // 2, 128)
-        packed = jnp.where(lane[:ITEM // 2] < 64, lo, pltpu.roll(hi, 64, axis=1))
+    def begin(d, dc, passed):
+        for t in range(2):
+            @pl.when(passed != 0)
+            def _():
+                g_copy(t, group(t, passed, 0), sibling, f_s.at[t, 0]).wait_recv()
+                sibling_copy(t, passed).start()
+
+            @pl.when(dc == 1)
+            def _():
+                g_copy(t, group(t, d, 1), sibling, f_s.at[t, 0]).wait_recv()
+
+    def end(packed, d, dc, added):
+        half = ITEM // 2
 
         @pl.when(dc == 0)
         def _():
-            keep[t, d] = packed
+            for t in range(2):
+                keep[t, d] = packed[t * half:(t + 1) * half]
 
         @pl.when(dc == 1)
         def _():
-            core_out[t, d] = packed.astype(BF16)
-            core_copy(t, d).start()
-
-        before = 1 - t
-        bd, bdc = lookup(s - 1, 0), lookup(s - 1, 1)
-
-        @pl.when(jnp.logical_and(bdc == 1, bd != 0))
+            for t in range(2):
+                core_out[t, d] = packed[t * half:(t + 1) * half].astype(BF16)
+                core_copy(t, d).start()
+
+        @pl.when(added != 0)
         def _():
-            core_copy(before, bd).wait_recv()
-            axis_out[before, bd] = (keep[before, bd] + core_in[before, bd].astype(F32)).astype(BF16)
-            part_copy(before, bd).start()
-
+            for t in range(2):
+                core_copy(t, added).wait_recv()
+                axis_out[t, added] = (keep[t, added] + core_in[t, added].astype(F32)).astype(BF16)
+                part_copy(t, added).start()
+
+    def step(s, _):
+        d, dc = look([o[0] for o in ORDER], s), look([o[1] for o in ORDER], s)
+
+        @pl.when(s == 1)
+        def _():
+            for t in range(2):
+                axis_copy(t, 2).start()
+
+        begin(d, dc, look(PASS_ON, s))
+        r = groups(group(0, d, dc), group(1, d, dc))
+        end(pack(products(r), r), d, dc, look(ADD_UP, s))
         return 0
 
-    lax.fori_loop(0, ITEMS, item, 0)
+    lax.fori_loop(0, len(ORDER), step, 0)
 
     grad = (acc_col[0:64] - acc_col[64:65] * cx[0:64].astype(F32)) * col_scale
     for p in range(8):
         block = grad[8 * p:8 * p + 8]
         back_out[p] = jnp.concatenate([block[:, :512], block[:, 512:]], axis=0).astype(BF16)
-
     back_start, back_forward, back_finish, back_sent = exchange(back_out, back_in, back_relay, back_s, back_r)
     back_start()
 
@@ -337,14 +335,14 @@
         for c in mm_copies[t]:
             c.start()
     back_forward()
-    halves = []
+    blocks = []
     for t in range(2):
         total = keep[t, 0, pl.ds(pl.multiple_of(place[t] * 64, 64), 64), :]
         for c, d in zip(mm_copies[t], range(1, 4)):
             c.wait_recv()
             total += mid_in[t, d].astype(F32)
-        halves.append(total.reshape(NZ, 8, 128))
-    z_out[...] = jnp.concatenate(halves, axis=1).astype(BF16)
+        blocks.append(total.reshape(NZ, 8, 128))
+    z_out[...] = jnp.concatenate(blocks, axis=1).astype(BF16)
 
     def zz_copy(d):
         return pltpu.make_async_remote_copy(
@@ -413,11 +411,9 @@
             pltpu.VMEM((8, 16, 768), BF16),
             pltpu.VMEM((8, 16, 768), BF16),
             pltpu.VMEM((4, 16, 768), BF16),
-            pltpu.VMEM((FEAT, TILE), BF16),
-            pltpu.VMEM((4 * FEAT, TILE), F8),
-            pltpu.VMEM((1, TILE), F32),
             pltpu.VMEM((128, TILE), BF16),
-            pltpu.VMEM((TILE, 128), BF16),
+            pltpu.VMEM((128, TILE), BF16),
+            pltpu.VMEM((TILE, 256), BF16),
             pltpu.VMEM((own_cols // 128, 128), F32),
             pltpu.VMEM((80, TILE), F32),
             pltpu.VMEM((2, 4, half, 128), F32),

time: 60.6 us -> 56.2 us (0.927)
  Pallas kernels: 56.8 us -> 52.2 us
    pallas_call x1, Pallas kernels: 56.8 us -> 52.2 us  [body(): pl.pallas_call(functools.partial(kernel, 1.0 / points ** 0.5, 1.0 / windo...]
where the time goes in v3:
time: 56.2 us; the launch traced here: 55.9 us
  Pallas kernels  52.2 us (93%)
  local copies, waits for them, and re-layouts  2.99 us (5%)
  between operations  0.64 us (1%)
    pallas_call x1, Pallas kernels, body(): pl.pallas_call(functools.partial(kernel, 1.0 / points ** 0.5, 1.0 / windo...  52.2 us
    unnamed x2, local copies, waits for them, and re-layouts  2.99 us

profile of v3, /device:TPU:2, one launch (start us, length us, event | category | flops | bytes accessed | tf_op | source)
XLA Modules:
  0.0 55.9 jit_solution(5603286644886073123)
XLA Ops:
  0.6 52.2 %evidence_gradients.1 = (f32[32,64]{1,0:T(8,128)}, f32[8,8192]{1,0:T(8,128)}) custom-call(bf16[32,64]{1,0:T(8,128)(2,1)} %bitcast.8, bf16[1,32]{1,0:T(2,128)(2,1)} %bitcast.9, bf16[32,32]{1,0:T(8,128)(2,1)} %rs_hbm.1, bf16[8,8192]{1,0:T(8,128)(2,1)} %cf_hbm.1, bf16[64,128]{1,0:T(8,128)(2,1)} %bitcast.6, f32[64,128]{1,0:T(8,128)} %bitcast.5, ...), custom_call_target="tpu_custom_call" | custom-call | tf_op jit(solution)/shard_map/evidence_gradients/pallas_call | solution.py:398
  52.9 1.3 %copy.11 = f32[64,32]{0,1:T(8,128)} copy(f32[64,32]{0,1:T(8,128)} %bitcast.7) | data formatting | bytes 16384
  54.2 1.7 %copy.12 = f32[8,8192]{1,0:T(8,128)} copy(f32[8,8192]{1,0:T(8,128)} %get-tuple-element.9) | data formatting | bytes 524288

commit v4 on v3

--- a/solution.py
+++ b/solution.py
@@ -9,6 +9,8 @@
 
 MESH = pl.DeviceIdType.MESH
 F32 = jnp.float32
+FAR = (2, 1, 3)
+FAR_Z = (4, 3, 5, 2, 6, 1, 7)
 BF16 = jnp.bfloat16
 
 FEAT = 64
@@ -18,9 +20,18 @@
 ITEM = 512
 HALF = 16
 
-ORDER = ((0, 1), (1, 0), (1, 1), (3, 1), (3, 0), (2, 1), (2, 0), (0, 0))
-PASS_ON = (0, 1, 3, 0, 2, 0, 0, 0)
-ADD_UP = (0, 0, 0, 1, 3, 0, 2, 0)
+STEPS = (
+    ((0, 0), (1, 0), 1),
+    ((0, 1), (0, 3), 0),
+    ((0, 1), (0, 3), 1),
+    ((1, 1), (1, 3), 0),
+    ((1, 1), (1, 3), 1),
+    ((0, 2), (1, 2), 1),
+    ((0, 2), (1, 2), 0),
+    ((0, 0), (1, 0), 0),
+)
+PASS_ON = {1: 1, 3: 3, 4: 6}
+ADD_UP = {3: 1, 5: 3, 6: 6}
 
 
 def look(values, at):
@@ -39,11 +50,11 @@
 def kernel(
     row_scale, col_scale,
     rf_hbm, ra_hbm, rs_hbm, cf_hbm, ca_hbm, cw_hbm, cp_hbm,
-    out_rows, out_cols,
+    out_rows, back_in,
     rf_ref, ra_ref, rs_ref, cf_ref, ca_ref, cw_ref, cp_ref, in_s,
     zbuf, rows, send_cols, recv_cols, relay, cx, cr, xct, small, acc_col,
     keep, core_out, core_in, axis_out, axis_in,
-    mid_out, mid_in, z_out, z_in, back_out, back_in, back_relay,
+    mid_out, mid_in, z_out, z_in, back_out, back_relay,
     col_s, col_r, z_s, z_r, m_s, m_r, g_s, g_r, f_s,
     core_s, core_r, axis_s, axis_r, mm_s, mm_r, zz_s, zz_r, back_s, back_r,
 ):
@@ -92,8 +103,8 @@
                 c.start()
             into[row] = out[row]
 
-        def forward():
-            for a, b in zip(first, third):
+        def forward(begin, end):
+            for a, b in zip(first[begin:end], third[begin:end]):
                 a.wait_recv()
                 b.start()
 
@@ -189,7 +200,7 @@
     def sibling_copy(t, d):
         return g_copy(t, group(t, d, 0), sibling, f_s.at[t, d])
 
-    z_copies = [z_copy(d) for d in range(1, NZ)]
+    z_copies = [z_copy(d) for d in FAR_Z]
     for c in z_copies:
         c.start()
     col_start, col_forward, col_finish, col_sent = exchange(send_cols, recv_cols, relay, col_s, col_r)
@@ -199,16 +210,18 @@
     m_copies = []
     for t in range(2):
         rows[t, own[t], place[t]] = zbuf[:, t * HALF:(t + 1) * HALF]
-        m_copies.append([m_copy(t, d) for d in range(1, 4)])
+        m_copies.append([m_copy(t, d) for d in FAR])
         for c in m_copies[t]:
             c.start()
-    col_forward()
+    col_forward(0, 3)
     for t in range(2):
         for c in m_copies[t]:
             c.wait_recv()
         sibling_copy(t, 0).start()
-        axis_copy(t, 1).start()
-        axis_copy(t, 3).start()
+    for d in (1, 3):
+        axis_copy(0, d).start()
+    for d in (1, 3):
+        axis_copy(1, d).start()
     col_finish()
 
     feats = jnp.concatenate(
@@ -232,9 +245,6 @@
 
     low = lax.broadcasted_iota(jnp.int32, (ITEM, 128), 1) < 64
 
-    def groups(g0, g1):
-        return jnp.concatenate([rows[0, g0].reshape(ITEM, 128), rows[1, g1].reshape(ITEM, 128)], axis=0)
-
     def products(r):
         cross = jnp.dot(r, cx[...], preferred_element_type=F32)
         weights = jnp.dot(r, cr[...], preferred_element_type=F32)
@@ -263,52 +273,62 @@
             src_ref=axis_out.at[t, d], dst_ref=axis_in.at[t, d],
             send_sem=axis_s.at[t, d], recv_sem=axis_r.at[t, d], device_id=axis_peer(t, d), device_id_type=MESH)
 
-    def begin(d, dc, passed):
-        for t in range(2):
-            @pl.when(passed != 0)
-            def _():
-                g_copy(t, group(t, passed, 0), sibling, f_s.at[t, 0]).wait_recv()
-                sibling_copy(t, passed).start()
-
-            @pl.when(dc == 1)
-            def _():
+    def pairs(s):
+        return [[look([o[k][i] for o in STEPS], s) for i in range(2)] for k in range(2)]
+
+    def some(table, s):
+        return look([table.get(k, -1) for k in range(len(STEPS))], s)
+
+    def begin(s, two, dc):
+        passed = some(PASS_ON, s)
+
+        @pl.when(passed >= 0)
+        def _():
+            for t, d in pairs(passed):
+                g_copy(t, group(t, d, 0), sibling, f_s.at[t, 0]).wait_recv()
+                sibling_copy(t, d).start()
+
+        @pl.when(dc == 1)
+        def _():
+            for t, d in two:
                 g_copy(t, group(t, d, 1), sibling, f_s.at[t, 0]).wait_recv()
 
-    def end(packed, d, dc, added):
+    def end(packed, s, two, dc):
         half = ITEM // 2
+        added = some(ADD_UP, s)
 
         @pl.when(dc == 0)
         def _():
-            for t in range(2):
-                keep[t, d] = packed[t * half:(t + 1) * half]
+            for k, (t, d) in enumerate(two):
+                keep[t, d] = packed[k * half:(k + 1) * half]
 
         @pl.when(dc == 1)
         def _():
-            for t in range(2):
-                core_out[t, d] = packed[t * half:(t + 1) * half].astype(BF16)
+            for k, (t, d) in enumerate(two):
+                core_out[t, d] = packed[k * half:(k + 1) * half].astype(BF16)
                 core_copy(t, d).start()
 
-        @pl.when(added != 0)
-        def _():
-            for t in range(2):
-                core_copy(t, added).wait_recv()
-                axis_out[t, added] = (keep[t, added] + core_in[t, added].astype(F32)).astype(BF16)
-                part_copy(t, added).start()
+        @pl.when(added >= 0)
+        def _():
+            for t, d in pairs(added):
+                core_copy(t, d).wait_recv()
+                axis_out[t, d] = (keep[t, d] + core_in[t, d].astype(F32)).astype(BF16)
+                part_copy(t, d).start()
 
     def step(s, _):
-        d, dc = look([o[0] for o in ORDER], s), look([o[1] for o in ORDER], s)
+        two, dc = pairs(s), look([o[2] for o in STEPS], s)
 
         @pl.when(s == 1)
         def _():
             for t in range(2):
                 axis_copy(t, 2).start()
 
-        begin(d, dc, look(PASS_ON, s))
-        r = groups(group(0, d, dc), group(1, d, dc))
-        end(pack(products(r), r), d, dc, look(ADD_UP, s))
+        begin(s, two, dc)
+        r = jnp.concatenate([rows[t, group(t, d, dc)].reshape(ITEM, 128) for t, d in two], axis=0)
+        end(pack(products(r), r), s, two, dc)
         return 0
 
-    lax.fori_loop(0, len(ORDER), step, 0)
+    lax.fori_loop(0, len(STEPS), step, 0)
 
     grad = (acc_col[0:64] - acc_col[64:65] * cx[0:64].astype(F32)) * col_scale
     for p in range(8):
@@ -331,14 +351,14 @@
             total += axis_in[t, d].astype(F32)
         keep[t, 0] = total
         mid_out[t] = total.reshape(4, 64, 128).astype(BF16)
-        mm_copies.append([mm_copy(t, d) for d in range(1, 4)])
+        mm_copies.append([mm_copy(t, d) for d in FAR])
         for c in mm_copies[t]:
             c.start()
-    back_forward()
+
     blocks = []
     for t in range(2):
         total = keep[t, 0, pl.ds(pl.multiple_of(place[t] * 64, 64), 64), :]
-        for c, d in zip(mm_copies[t], range(1, 4)):
+        for c, d in zip(mm_copies[t], FAR):
             c.wait_recv()
             total += mid_in[t, d].astype(F32)
         blocks.append(total.reshape(NZ, 8, 128))
@@ -349,23 +369,16 @@
             src_ref=z_out.at[(z + d) % NZ], dst_ref=z_in.at[d],
             send_sem=zz_s.at[d], recv_sem=zz_r.at[d], device_id=z_peer(d), device_id_type=MESH)
 
-    zz_copies = [zz_copy(d) for d in range(1, NZ)]
+    zz_copies = [zz_copy(d) for d in FAR_Z]
     for c in zz_copies:
         c.start()
+    back_forward(0, 3)
     total = z_out[z].astype(F32)
-    for c, d in zip(zz_copies, range(1, NZ)):
+    for c, d in zip(zz_copies, FAR_Z):
         c.wait_recv()
         total += z_in[d].astype(F32)
-    total = total * row_scale
-    moved = pltpu.roll(total, 64, axis=1)
-    final = jnp.concatenate([total[0:8], moved[0:8], total[8:16], moved[8:16]], axis=0)
-    out_rows[...] = final[:, 0:64]
-
+    out_rows[...] = total * row_scale
     back_finish()
-    for p in range(8):
-        block = back_in[p].astype(F32)
-        out_cols[:, p * TILE:p * TILE + 512] = block[0:8]
-        out_cols[:, p * TILE + 512:(p + 1) * TILE] = block[8:16]
 
     col_sent()
     back_sent()
@@ -378,6 +391,17 @@
             if d:
                 axis_copy(t, d).wait_send()
                 part_copy(t, d).wait_send()
+
+
+def unpack(rows_ref, cols_ref, out_rows, out_cols):
+    total = rows_ref[...]
+    moved = pltpu.roll(total, 64, axis=1)
+    final = jnp.concatenate([total[0:8], moved[0:8], total[8:16], moved[8:16]], axis=0)
+    out_rows[...] = final[:, 0:64]
+    for p in range(8):
+        block = cols_ref[p].astype(F32)
+        out_cols[:, p * TILE:p * TILE + 512] = block[0:8]
+        out_cols[:, p * TILE + 512:(p + 1) * TILE] = block[8:16]
 
 
 def body(row_feats, row_alpha, row_solves, col_feats, col_alpha, col_weight, col_probes):
@@ -395,11 +419,11 @@
         col_alpha.reshape(-1, 128), col_weight.reshape(-1, 128), col_probes,
     )
     half = ITEM // 2
-    grad_rows, grad_cols = pl.pallas_call(
+    totals = pl.pallas_call(
         functools.partial(kernel, 1.0 / points**0.5, 1.0 / window**0.5),
         out_shape=(
-            jax.ShapeDtypeStruct((own_rows, FEAT), F32),
-            jax.ShapeDtypeStruct((FEAT // row_size, own_cols), F32),
+            jax.ShapeDtypeStruct((16, 128), F32),
+            jax.ShapeDtypeStruct((8, 16, 512), BF16),
         ),
         in_specs=[hbm] * 7,
         out_specs=(vmem, vmem),
@@ -420,7 +444,7 @@
             *[pltpu.VMEM((2, 4, half, 128), BF16)] * 4,
             *[pltpu.VMEM((2, 4, half // 4, 128), BF16)] * 2,
             *[pltpu.VMEM((NZ, 16, 128), BF16)] * 2,
-            *[pltpu.VMEM((8, 16, 512), BF16)] * 2,
+            pltpu.VMEM((8, 16, 512), BF16),
             pltpu.VMEM((4, 16, 512), BF16),
             dma((3, 4)), dma((3, 4)), dma((NZ,)), dma((NZ,)), dma((2, 4)), dma((2, 4)),
             dma((2, 4)), dma((2, 8)), dma((2, 4)),
@@ -431,6 +455,16 @@
             collective_id=0, has_side_effects=True, vmem_limit_bytes=63 * 2**20),
         name="evidence_gradients",
     )(*args)
+    grad_rows, grad_cols = pl.pallas_call(
+        unpack,
+        out_shape=(
+            jax.ShapeDtypeStruct((own_rows, FEAT), F32),
+            jax.ShapeDtypeStruct((FEAT // row_size, own_cols), F32),
+        ),
+        in_specs=[vmem] * 2,
+        out_specs=(vmem, vmem),
+        name="unpack_gradients",
+    )(*totals)
     return grad_rows.T, grad_cols
 
 

time: 56.2 us -> 53.3 us (0.948)
  local copies, waits for them, and re-layouts: 2.99 us -> 0 us
    unnamed x2 -> x0, local copies, waits for them, and re-layouts: 2.99 us -> none
    pallas_call x0 -> x1, Pallas kernels: none -> 1.64 us  [body(): pl.pallas_call(unpack, out_shape=(jax.ShapeDtypeStruct((own_rows, FEAT),...]
    pallas_call x1, Pallas kernels: 52.2 us -> 50.6 us  [body(): pl.pallas_call(functools.partial(kernel, 1.0 / points ** 0.5, 1.0 / windo...]
where the time goes in v4:
time: 53.3 us; the launch traced here: 52.9 us
  Pallas kernels  52.3 us (98%)
  between operations  0.64 us (1%)
    pallas_call x1, Pallas kernels, body(): pl.pallas_call(functools.partial(kernel, 1.0 / points ** 0.5, 1.0 / windo...  50.6 us
    pallas_call x1, Pallas kernels, body(): pl.pallas_call(unpack, out_shape=(jax.ShapeDtypeStruct((own_rows, FEAT),...  1.64 us

profile of v4, /device:TPU:2, one launch (start us, length us, event | category | flops | bytes accessed | tf_op | source)
XLA Modules:
  0.0 52.9 jit_solution(907592989135272772)
XLA Ops:
  0.6 50.6 %evidence_gradients.1 = (f32[16,128]{1,0:T(8,128)}, bf16[8,16,512]{2,1,0:T(8,128)(2,1)}) custom-call(bf16[32,64]{1,0:T(8,128)(2,1)} %bitcast.7, bf16[1,32]{1,0:T(2,128)(2,1)} %bitcast.8, bf16[32,32]{1,0:T(8,128)(2,1)} %rs_hbm.1, bf16[8,8192]{1,0:T(8,128)(2,1)} %cf_hbm.1, bf16[64,128]{1,0:T(8,128)(2,1)} %bitcast.6, f32[64,128]{1,0:T(8,128)} %bitcast.5, ...), custom_call_target="tpu_custom_call" | custom-call | tf_op jit(solution)/shard_map/evidence_gradients/pallas_call | solution.py:422
  51.3 1.6 %unpack_gradients.1 = (f32[32,64]{1,0:T(8,128)}, f32[8,8192]{1,0:T(8,128)}) custom-call(f32[16,128]{1,0:T(8,128)} %get-tuple-element.6.rows_ref, bf16[8,16,512]{2,1,0:T(8,128)(2,1)} %get-tuple-element.7.cols_ref), custom_call_target="tpu_custom_call" | custom-call | tf_op jit(solution)/shard_map/unpack_gradients/pallas_call | solution.py:458

commit v5 on v4

--- a/solution.py
+++ b/solution.py
@@ -48,13 +48,13 @@
 
 
 def kernel(
-    row_scale, col_scale,
+    col_scale,
     rf_hbm, ra_hbm, rs_hbm, cf_hbm, ca_hbm, cw_hbm, cp_hbm,
-    out_rows, back_in,
+    z_in, back_in,
     rf_ref, ra_ref, rs_ref, cf_ref, ca_ref, cw_ref, cp_ref, in_s,
     zbuf, rows, send_cols, recv_cols, relay, cx, cr, xct, small, acc_col,
     keep, core_out, core_in, axis_out, axis_in,
-    mid_out, mid_in, z_out, z_in, back_out, back_relay,
+    mid_out, mid_in, z_out, back_out, back_relay,
     col_s, col_r, z_s, z_r, m_s, m_r, g_s, g_r, f_s,
     core_s, core_r, axis_s, axis_r, mm_s, mm_r, zz_s, zz_r, back_s, back_r,
 ):
@@ -98,10 +98,12 @@
         second = [over_y(d) for d in (2, 1, 3)]
         third = [onward(d) for d in (2, 1, 3)]
 
+        mine = pltpu.make_async_copy(out.at[row], into.at[row], send.at[1, 0])
+
         def start():
             for c in first + second:
                 c.start()
-            into[row] = out[row]
+            mine.start()
 
         def forward(begin, end):
             for a, b in zip(first[begin:end], third[begin:end]):
@@ -111,6 +113,7 @@
         def finish():
             for c in second + [first[3]] + third:
                 c.wait_recv()
+            mine.wait()
 
         def sent():
             for c in first + second + third:
@@ -124,14 +127,13 @@
             (rf_hbm, rf_ref), (ra_hbm, ra_ref), (rs_hbm, rs_ref), (cf_hbm, cf_ref),
             (cp_hbm, cp_ref), (ca_hbm, ca_ref), (cw_hbm, cw_ref)))
     ]
+    barrier = pltpu.get_barrier_semaphore()
+    peers = [z_peer(d) for d in FAR_Z]
+    peers += [axis_peer(t, d) for t in range(2) for d in FAR] + [sibling]
+    for peer in peers:
+        pl.semaphore_signal(barrier, inc=1, device_id=peer, device_id_type=MESH)
     for c in loads:
         c.start()
-
-    barrier = pltpu.get_barrier_semaphore()
-    peers = [z_peer(d) for d in range(1, NZ)] + [sibling]
-    peers += [axis_peer(t, d) for t in range(2) for d in range(1, 4)]
-    for peer in peers:
-        pl.semaphore_signal(barrier, inc=1, device_id=peer, device_id_type=MESH)
 
     for c in loads[:3]:
         c.wait()
@@ -372,12 +374,12 @@
     zz_copies = [zz_copy(d) for d in FAR_Z]
     for c in zz_copies:
         c.start()
+    mine = pltpu.make_async_copy(z_out.at[z], z_in.at[0], zz_s.at[0])
+    mine.start()
     back_forward(0, 3)
-    total = z_out[z].astype(F32)
-    for c, d in zip(zz_copies, FAR_Z):
+    for c in zz_copies:
         c.wait_recv()
-        total += z_in[d].astype(F32)
-    out_rows[...] = total * row_scale
+    mine.wait()
     back_finish()
 
     col_sent()
@@ -393,8 +395,11 @@
                 part_copy(t, d).wait_send()
 
 
-def unpack(rows_ref, cols_ref, out_rows, out_cols):
-    total = rows_ref[...]
+def unpack(row_scale, rows_ref, cols_ref, out_rows, out_cols):
+    total = rows_ref[0].astype(F32)
+    for d in range(1, NZ):
+        total += rows_ref[d].astype(F32)
+    total = total * row_scale
     moved = pltpu.roll(total, 64, axis=1)
     final = jnp.concatenate([total[0:8], moved[0:8], total[8:16], moved[8:16]], axis=0)
     out_rows[...] = final[:, 0:64]
@@ -420,13 +425,13 @@
     )
     half = ITEM // 2
     totals = pl.pallas_call(
-        functools.partial(kernel, 1.0 / points**0.5, 1.0 / window**0.5),
+        functools.partial(kernel, 1.0 / window**0.5),
         out_shape=(
-            jax.ShapeDtypeStruct((16, 128), F32),
+            jax.ShapeDtypeStruct((NZ, 16, 128), BF16),
             jax.ShapeDtypeStruct((8, 16, 512), BF16),
         ),
         in_specs=[hbm] * 7,
-        out_specs=(vmem, vmem),
+        out_specs=(hbm, hbm),
         scratch_shapes=[
             *[pltpu.VMEM(a.shape, a.dtype) for a in args],
             dma((7,)),
@@ -443,7 +448,7 @@
             pltpu.VMEM((2, 4, half, 128), F32),
             *[pltpu.VMEM((2, 4, half, 128), BF16)] * 4,
             *[pltpu.VMEM((2, 4, half // 4, 128), BF16)] * 2,
-            *[pltpu.VMEM((NZ, 16, 128), BF16)] * 2,
+            pltpu.VMEM((NZ, 16, 128), BF16),
             pltpu.VMEM((8, 16, 512), BF16),
             pltpu.VMEM((4, 16, 512), BF16),
             dma((3, 4)), dma((3, 4)), dma((NZ,)), dma((NZ,)), dma((2, 4)), dma((2, 4)),
@@ -456,7 +461,7 @@
         name="evidence_gradients",
     )(*args)
     grad_rows, grad_cols = pl.pallas_call(
-        unpack,
+        functools.partial(unpack, 1.0 / points**0.5),
         out_shape=(
             jax.ShapeDtypeStruct((own_rows, FEAT), F32),
             jax.ShapeDtypeStruct((FEAT // row_size, own_cols), F32),

time: 53.3 us -> 52.7 us (0.989)
  Pallas kernels: 52.3 us -> 51.7 us
    pallas_call x2, Pallas kernels: 52.3 us -> 51.7 us  [the longest x1 50.1 us: body(): pl.pallas_call(functools.partial(kernel, 1.0 / window ** 0.5), out_shape=...]
where the time goes in v5:
time: 52.7 us; the launch traced here: 52.4 us
  Pallas kernels  51.7 us (98%)
  between operations  0.64 us (1%)
    pallas_call x1, Pallas kernels, body(): pl.pallas_call(functools.partial(kernel, 1.0 / window ** 0.5), out_shape=...  50.1 us
    pallas_call x1, Pallas kernels, body(): pl.pallas_call(functools.partial(unpack, 1.0 / points ** 0.5), out_shape=...  1.65 us

profile of v5, /device:TPU:2, one launch (start us, length us, event | category | flops | bytes accessed | tf_op | source)
XLA Modules:
  0.0 52.4 jit_solution(10787441563149897042)
XLA Ops:
  0.6 50.1 %evidence_gradients.1 = (bf16[8,16,128]{2,1,0:T(8,128)(2,1)}, bf16[8,16,512]{2,1,0:T(8,128)(2,1)}) custom-call(bf16[32,64]{1,0:T(8,128)(2,1)} %bitcast.7, bf16[1,32]{1,0:T(2,128)(2,1)} %bitcast.8, bf16[32,32]{1,0:T(8,128)(2,1)} %rs_hbm.1, bf16[8,8192]{1,0:T(8,128)(2,1)} %cf_hbm.1, bf16[64,128]{1,0:T(8,128)(2,1)} %bitcast.6, f32[64,128]{1,0:T(8,128)} %bitcast.5, ...), custom_call_target="tpu_custom_call" | custom-call | tf_op jit(solution)/shard_map/evidence_gradients/pallas_call | solution.py:427
  50.7 1.7 %unpack_gradients.1 = (f32[32,64]{1,0:T(8,128)}, f32[8,8192]{1,0:T(8,128)}) custom-call(bf16[8,16,128]{2,1,0:T(8,128)(2,1)} %get-tuple-element.6.rows_ref, bf16[8,16,512]{2,1,0:T(8,128)(2,1)} %get-tuple-element.7.cols_ref), custom_call_target="tpu_custom_call" | custom-call | tf_op jit(solution)/shard_map/unpack_gradients/pallas_call | solution.py:463

commit v6 on v5

--- a/solution.py
+++ b/solution.py
@@ -24,14 +24,14 @@
     ((0, 0), (1, 0), 1),
     ((0, 1), (0, 3), 0),
     ((0, 1), (0, 3), 1),
-    ((1, 1), (1, 3), 0),
     ((1, 1), (1, 3), 1),
     ((0, 2), (1, 2), 1),
     ((0, 2), (1, 2), 0),
+    ((1, 1), (1, 3), 0),
     ((0, 0), (1, 0), 0),
 )
-PASS_ON = {1: 1, 3: 3, 4: 6}
-ADD_UP = {3: 1, 5: 3, 6: 6}
+PASS_ON = {1: 1, 2: 6, 3: 5}
+ADD_UP = {3: 1, 5: 5, 6: 6}
 
 
 def look(values, at):

time: 52.7 us -> 52.4 us (level)
  no operation moved by 1% of the time
where the time goes in v6:
time: 52.4 us; the launch traced here: 52.2 us
  Pallas kernels  51.5 us (98%)
  between operations  0.64 us (1%)
    pallas_call x1, Pallas kernels, body(): pl.pallas_call(functools.partial(kernel, 1.0 / window ** 0.5), out_shape=...  49.9 us
    pallas_call x1, Pallas kernels, body(): pl.pallas_call(functools.partial(unpack, 1.0 / points ** 0.5), out_shape=...  1.65 us

profile of v6, /device:TPU:2, one launch (start us, length us, event | category | flops | bytes accessed | tf_op | source)
XLA Modules:
  0.0 52.2 jit_solution(14808352935878859934)
XLA Ops:
  0.6 49.9 %evidence_gradients.1 = (bf16[8,16,128]{2,1,0:T(8,128)(2,1)}, bf16[8,16,512]{2,1,0:T(8,128)(2,1)}) custom-call(bf16[32,64]{1,0:T(8,128)(2,1)} %bitcast.7, bf16[1,32]{1,0:T(2,128)(2,1)} %bitcast.8, bf16[32,32]{1,0:T(8,128)(2,1)} %rs_hbm.1, bf16[8,8192]{1,0:T(8,128)(2,1)} %cf_hbm.1, bf16[64,128]{1,0:T(8,128)(2,1)} %bitcast.6, f32[64,128]{1,0:T(8,128)} %bitcast.5, ...), custom_call_target="tpu_custom_call" | custom-call | tf_op jit(solution)/shard_map/evidence_gradients/pallas_call | solution.py:427
  50.5 1.7 %unpack_gradients.1 = (f32[32,64]{1,0:T(8,128)}, f32[8,8192]{1,0:T(8,128)}) custom-call(bf16[8,16,128]{2,1,0:T(8,128)(2,1)} %get-tuple-element.6.rows_ref, bf16[8,16,512]{2,1,0:T(8,128)(2,1)} %get-tuple-element.7.cols_ref), custom_call_target="tpu_custom_call" | custom-call | tf_op jit(solution)/shard_map/unpack_gradients/pallas_call | solution.py:463

commit v7 on v6

--- a/solution.py
+++ b/solution.py
@@ -209,10 +209,10 @@
     col_start()
     for c in z_copies:
         c.wait_recv()
-    m_copies = []
-    for t in range(2):
+    m_copies = [None, None]
+    for t in (1, 0):
         rows[t, own[t], place[t]] = zbuf[:, t * HALF:(t + 1) * HALF]
-        m_copies.append([m_copy(t, d) for d in FAR])
+        m_copies[t] = [m_copy(t, d) for d in FAR]
         for c in m_copies[t]:
             c.start()
     col_forward(0, 3)

time: 52.4 us -> 52.4 us (level)
  no operation moved by 1% of the time
where the time goes in v7:
time: 52.4 us; the launch traced here: 52.3 us
  Pallas kernels  51.6 us (98%)
  between operations  0.64 us (1%)
    pallas_call x1, Pallas kernels, body(): pl.pallas_call(functools.partial(kernel, 1.0 / window ** 0.5), out_shape=...  50 us
    pallas_call x1, Pallas kernels, body(): pl.pallas_call(functools.partial(unpack, 1.0 / points ** 0.5), out_shape=...  1.65 us

profile of v7, /device:TPU:2, one launch (start us, length us, event | category | flops | bytes accessed | tf_op | source)
XLA Modules:
  0.0 52.3 jit_solution(6740720807302538740)
XLA Ops:
  0.6 50.0 %evidence_gradients.1 = (bf16[8,16,128]{2,1,0:T(8,128)(2,1)}, bf16[8,16,512]{2,1,0:T(8,128)(2,1)}) custom-call(bf16[32,64]{1,0:T(8,128)(2,1)} %bitcast.7, bf16[1,32]{1,0:T(2,128)(2,1)} %bitcast.8, bf16[32,32]{1,0:T(8,128)(2,1)} %rs_hbm.1, bf16[8,8192]{1,0:T(8,128)(2,1)} %cf_hbm.1, bf16[64,128]{1,0:T(8,128)(2,1)} %bitcast.6, f32[64,128]{1,0:T(8,128)} %bitcast.5, ...), custom_call_target="tpu_custom_call" | custom-call | tf_op jit(solution)/shard_map/evidence_gradients/pallas_call | solution.py:427
  50.6 1.7 %unpack_gradients.1 = (f32[32,64]{1,0:T(8,128)}, f32[8,8192]{1,0:T(8,128)}) custom-call(bf16[8,16,128]{2,1,0:T(8,128)(2,1)} %get-tuple-element.6.rows_ref, bf16[8,16,512]{2,1,0:T(8,128)(2,1)} %get-tuple-element.7.cols_ref), custom_call_target="tpu_custom_call" | custom-call | tf_op jit(solution)/shard_map/unpack_gradients/pallas_call | solution.py:463

commit v8 on v7

--- a/solution.py
+++ b/solution.py
@@ -101,9 +101,13 @@
         mine = pltpu.make_async_copy(out.at[row], into.at[row], send.at[1, 0])
 
         def start():
-            for c in first + second:
+            for c in first:
                 c.start()
             mine.start()
+
+        def along_y():
+            for c in second:
+                c.start()
 
         def forward(begin, end):
             for a, b in zip(first[begin:end], third[begin:end]):
@@ -119,7 +123,7 @@
             for c in first + second + third:
                 c.wait_send()
 
-        return start, forward, finish, sent
+        return start, along_y, forward, finish, sent
 
     loads = [
         pltpu.make_async_copy(src, dst, in_s.at[k])
@@ -205,8 +209,9 @@
     z_copies = [z_copy(d) for d in FAR_Z]
     for c in z_copies:
         c.start()
-    col_start, col_forward, col_finish, col_sent = exchange(send_cols, recv_cols, relay, col_s, col_r)
+    col_start, col_along_y, col_forward, col_finish, col_sent = exchange(send_cols, recv_cols, relay, col_s, col_r)
     col_start()
+    col_along_y()
     for c in z_copies:
         c.wait_recv()
     m_copies = [None, None]
@@ -336,7 +341,7 @@
     for p in range(8):
         block = grad[8 * p:8 * p + 8]
         back_out[p] = jnp.concatenate([block[:, :512], block[:, 512:]], axis=0).astype(BF16)
-    back_start, back_forward, back_finish, back_sent = exchange(back_out, back_in, back_relay, back_s, back_r)
+    back_start, back_along_y, back_forward, back_finish, back_sent = exchange(back_out, back_in, back_relay, back_s, back_r)
     back_start()
 
     def mm_copy(t, d):
@@ -357,6 +362,7 @@
         for c in mm_copies[t]:
             c.start()
 
+    back_along_y()
     blocks = []
     for t in range(2):
         total = keep[t, 0, pl.ds(pl.multiple_of(place[t] * 64, 64), 64), :]

time: 52.4 us -> 52.4 us (level)
  no operation moved by 1% of the time
where the time goes in v8:
time: 52.4 us; the launch traced here: 52.3 us
  Pallas kernels  51.6 us (98%)
  between operations  0.64 us (1%)
    pallas_call x1, Pallas kernels, body(): pl.pallas_call(functools.partial(kernel, 1.0 / window ** 0.5), out_shape=...  50 us
    pallas_call x1, Pallas kernels, body(): pl.pallas_call(functools.partial(unpack, 1.0 / points ** 0.5), out_shape=...  1.65 us

profile of v8, /device:TPU:2, one launch (start us, length us, event | category | flops | bytes accessed | tf_op | source)
XLA Modules:
  0.0 52.3 jit_solution(6242553832575088627)
XLA Ops:
  0.6 50.0 %evidence_gradients.1 = (bf16[8,16,128]{2,1,0:T(8,128)(2,1)}, bf16[8,16,512]{2,1,0:T(8,128)(2,1)}) custom-call(bf16[32,64]{1,0:T(8,128)(2,1)} %bitcast.7, bf16[1,32]{1,0:T(2,128)(2,1)} %bitcast.8, bf16[32,32]{1,0:T(8,128)(2,1)} %rs_hbm.1, bf16[8,8192]{1,0:T(8,128)(2,1)} %cf_hbm.1, bf16[64,128]{1,0:T(8,128)(2,1)} %bitcast.6, f32[64,128]{1,0:T(8,128)} %bitcast.5, ...), custom_call_target="tpu_custom_call" | custom-call | tf_op jit(solution)/shard_map/evidence_gradients/pallas_call | solution.py:433
  50.6 1.7 %unpack_gradients.1 = (f32[32,64]{1,0:T(8,128)}, f32[8,8192]{1,0:T(8,128)}) custom-call(bf16[8,16,128]{2,1,0:T(8,128)(2,1)} %get-tuple-element.6.rows_ref, bf16[8,16,512]{2,1,0:T(8,128)(2,1)} %get-tuple-element.7.cols_ref), custom_call_target="tpu_custom_call" | custom-call | tf_op jit(solution)/shard_map/unpack_gradients/pallas_call | solution.py:469
